TPU v7x, 32 devices: a whole 2x2x4 slice. The times are simulated.
32 devices in a mesh: dp: 4 (over y, x), expert: 4 (over z), tensor: 2 (over core).
Axes of the slice: x: 2, y: 2, z: 4, core: 2. Of those that a mesh axis runs over, the one named last changes fastest.
Arguments:
- weight: bfloat16 [4, 1536, 4096], P('expert', 'tensor'), may hold values from -1.796875 to 1.796875
- factor_a: float32 [4, 64, 4096], P('expert', 'dp', 'tensor'), may hold values from -1.2 to 1.2
- factor_b: float32 [4, 64, 1536], P('expert', 'dp', 'tensor'), may hold values from -1.2 to 1.2
- moment_a: float32 [4, 64, 4096], P('expert', 'dp', 'tensor'), may hold values from -0.6 to 0.6
- second_a: float32 [4, 64, 4096], P('expert', 'dp', 'tensor'), may hold values from 0.003 to 1
- first_moment_factor_b: float32 [4, 64, 1536], P('expert', 'dp', 'tensor'), may hold values from -0.6 to 0.6
- second_b: float32 [4, 64, 1536], P('expert', 'dp', 'tensor'), may hold values from 0.003 to 1
- grad_a: float32 [4, 4, 64, 4096], P('dp', 'expert', None, 'tensor'), may hold values from -2 to 2
- grad_b: float32 [4, 4, 64, 1536], P('dp', 'expert', None, 'tensor'), may hold values from -2 to 2
- slot_of: int32 [4], replicated, may hold values from 0 to 3, each once
Outputs:
- merged: bfloat16 [4, 1536, 4096], P('expert', 'tensor')
- new_a: float32 [4, 64, 4096], P('expert', 'dp', 'tensor')
- new_b: float32 [4, 64, 1536], P('expert', 'dp', 'tensor')
- new_moment_a: float32 [4, 64, 4096], P('expert', 'dp', 'tensor')
- new_second_a: float32 [4, 64, 4096], P('expert', 'dp', 'tensor')
- new_moment_b: float32 [4, 64, 1536], P('expert', 'dp', 'tensor')
- new_second_b: float32 [4, 64, 1536], P('expert', 'dp', 'tensor')
Inputs may be any that keep to these rules, and one draw needn't show every extreme that they name: slot_of is a permutation; slot s belongs to the index s // 1 of expert.
All inputs are finite; a program needn't handle non-finite values.
Results may differ from a plain program's by a relative error of at most 0.0065.
Values may be sent and summed in bfloat16 or wider, within the bound.
No kernel may reach another device: no remote copies, remote signals or barrier semaphores. Data moves between devices by JAX's collectives and lax.ppermute only.
A program may use at most 64 MiB of HBM per device.

v0:
```python
import functools
import itertools

import jax
import jax.numpy as jnp
from jax import lax
from jax.experimental import pallas as pl
from jax.experimental.pallas import tpu as pltpu
from jax.sharding import PartitionSpec as P

ADAM_STEP = 20


ADAPTER_SCALE = 2.0
BETA_ONE = 0.9
BETA_TWO = 0.95
LEARN_RATE = 0.08
STABILITY_TERM = 1e-08

MOST_SWITCHED = 4

F32 = jnp.float32
BF16 = jnp.bfloat16
VMEM = pl.BlockSpec(memory_space=pltpu.VMEM)
SMEM = pl.BlockSpec(memory_space=pltpu.SMEM)
HBM = pl.BlockSpec(memory_space=pltpu.HBM)
PARAMS = pltpu.CompilerParams(vmem_limit_bytes=16 * 1024 * 1024)


def adam_update(param, moment, second, grad):
    corr_one = 1.0 - BETA_ONE**ADAM_STEP
    corr_two = 1.0 - BETA_TWO**ADAM_STEP
    moment_new = BETA_ONE * moment + (1.0 - BETA_ONE) * grad
    second_new = BETA_TWO * second + (1.0 - BETA_TWO) * grad * grad
    param_new = param - LEARN_RATE * (moment_new / corr_one) / (
        jnp.sqrt(second_new / corr_two) + STABILITY_TERM
    )
    return (param_new, moment_new, second_new)


def swap(x, axis, n, k):
    return lax.ppermute(x, axis, [(i, i ^ k) for i in range(n)])


def held(x):
    return pltpu.with_memory_space_constraint(x, pltpu.VMEM)


def left(x):
    return pltpu.with_memory_space_constraint(x, pltpu.HBM)


def estimate(nbytes, flops=0):
    return pl.CostEstimate(flops=flops, bytes_accessed=nbytes, transcendentals=0)


def pack_kernel(n_dp, ranks, cols_a, grad_a, grad_b, *refs):
    outs, rows, sems = refs[: n_dp - 1], refs[n_dp - 1], refs[n_dp]
    me = lax.axis_index("dp")
    copies = []
    for k in range(1, n_dp):
        start = pl.multiple_of((me ^ k) * ranks, ranks)
        pair = (
            pltpu.make_async_copy(
                grad_a.at[0, 0, pl.ds(start, ranks), :],
                rows.at[k - 1, :, pl.ds(0, cols_a)],
                sems.at[k - 1, 0],
            ),
            pltpu.make_async_copy(
                grad_b.at[0, 0, pl.ds(start, ranks), :],
                rows.at[k - 1, :, pl.ds(cols_a, rows.shape[2] - cols_a)],
                sems.at[k - 1, 1],
            ),
        )
        for copy in pair:
            copy.start()
        copies.append(pair)
    for k, pair in enumerate(copies):
        for copy in pair:
            copy.wait()
        outs[k][...] = rows[k].astype(BF16)


def load_kernel(ranks, cols_a, slots_in, *refs):
    grad_a, grad_b, fa, fb, ma, mb, sa, sb = refs[:8]
    grad, factor, moment, second, order, slot_of, sems = refs[8:]
    me = lax.axis_index("dp")
    start = pl.multiple_of(me * ranks, ranks)
    first = pl.ds(0, cols_a)
    last = pl.ds(cols_a, grad.shape[1] - cols_a)
    pairs = [
        (grad_a.at[0, 0, pl.ds(start, ranks), :], grad.at[:, first]),
        (grad_b.at[0, 0, pl.ds(start, ranks), :], grad.at[:, last]),
        (fa.at[0], factor.at[:, first]),
        (fb.at[0], factor.at[:, last]),
        (ma.at[0], moment.at[:, first]),
        (mb.at[0], moment.at[:, last]),
        (sa.at[0], second.at[:, first]),
        (sb.at[0], second.at[:, last]),
        (slots_in, slot_of),
    ]
    copies = [pltpu.make_async_copy(a, b, sems.at[i]) for i, (a, b) in enumerate(pairs)]
    for copy in copies:
        copy.start()
    copies.pop().wait()
    n = slot_of.shape[0]
    number = jnp.int32(0)
    for i in range(n - 1):
        smaller = jnp.int32(0)
        for j in range(i + 1, n):
            smaller += (slot_of[j] < slot_of[i]).astype(jnp.int32)
        number = number * (n - i) + smaller
    order[0] = number
    here = lax.axis_index("expert")
    order[1] = (slot_of[here] == here).astype(jnp.int32)
    for copy in copies:
        copy.wait()


def keep_kernel(piece, kept):
    kept[...] = piece[...]


def send_kernel(*refs):
    grad, factor, moment, second = refs[:4]
    total = grad[...]
    for piece in refs[4:-1]:
        total = total + piece[...].astype(F32)
    refs[-1][...] = adam_update(factor[...], moment[...], second[...], total)[0].astype(BF16)


def state_kernel(n_got, cols_a, weight, *refs):
    ins = refs[: 4 + n_got]
    outs = refs[4 + n_got : 10 + n_got]
    panel = refs[10 + n_got]
    parts = refs[11 + n_got : 17 + n_got]
    sems = refs[-1]
    cols_b = ins[0].shape[1] - cols_a
    width = 256 if cols_a % 256 == 0 and cols_b % 256 == 0 else 128
    load = pltpu.make_async_copy(weight.at[0], panel, sems.at[0])
    load.start()

    def some_columns(start, into, at):
        here = pl.ds(pl.multiple_of(start, width), width)
        there = pl.ds(pl.multiple_of(at, width), width)
        grad, factor, moment, second = (ref[:, here] for ref in ins[:4])
        for piece in ins[4:]:
            grad = grad + piece[:, here].astype(F32)
        for out, new in zip(into, adam_update(factor, moment, second, grad)):
            out[:, there] = new

    @pl.loop(0, cols_a // width)
    def _(i):
        some_columns(i * width, parts[::2], i * width)

    @pl.loop(0, cols_b // width)
    def _(i):
        some_columns(cols_a + i * width, parts[1::2], i * width)

    copies = [
        pltpu.make_async_copy(part, out.at[0], sems.at[1 + i])
        for i, (part, out) in enumerate(zip(parts, outs))
    ]
    for copy in copies:
        copy.start()
    for copy in copies:
        copy.wait()
    load.wait()


def join_kernel(cols_a, *refs):
    parts = refs[:-4]
    rows_a, flipped = refs[-3:-1]
    ranks = parts[0].shape[0]
    for i, part in enumerate(parts):
        rows_a[pl.ds(i * ranks, ranks), :] = part[:, :cols_a]
    rows_b = jnp.concatenate([part[:, cols_a:].astype(F32) for part in parts], axis=0)
    flipped[...] = (rows_b * ADAPTER_SCALE).T.astype(BF16)


def merge_kernel(k, width, *refs):
    panel, rows_a, flipped = refs[:3]
    out, tiles, sems = refs[-3:]
    cols = rows_a.shape[1]
    base = (lax.axis_index("tensor") ^ k) * cols
    copies = []
    for step in range(cols // width):
        span = slice(step * width, (step + 1) * width)
        columns = pl.ds(pl.multiple_of(base + step * width, width), width)
        increment = jnp.dot(flipped[...], rows_a[:, span], preferred_element_type=F32)
        tiles[step] = (panel[:, columns].astype(F32) + increment).astype(BF16)
        copy = pltpu.make_async_copy(tiles.at[step], out.at[0, :, columns], sems.at[step])
        copy.start()
        copies.append(copy)
    for copy in copies:
        copy.wait()


def per_device(
    n_dp,
    n_expert,
    n_tensor,
    weight,
    factor_a,
    factor_b,
    moment_a,
    second_a,
    first_moment_factor_b,
    second_b,
    grad_a,
    grad_b,
    slot_of,
):
    ranks, cols_a = factor_a.shape[1:]
    cols_b = factor_b.shape[2]
    cols = cols_a + cols_b

    pieces = pl.pallas_call(
        functools.partial(pack_kernel, n_dp, ranks, cols_a),
        in_specs=[HBM, HBM],
        out_specs=[VMEM] * (n_dp - 1),
        out_shape=[pltpu.VMEM((ranks, cols), BF16)] * (n_dp - 1),
        scratch_shapes=[
            pltpu.VMEM((n_dp - 1, ranks, cols), F32),
            pltpu.SemaphoreType.DMA((n_dp - 1, 2)),
        ],
        compiler_params=PARAMS,
        name="pack",
    )(left(grad_a), left(grad_b))
    got = [held(swap(pieces[k - 1], "dp", n_dp, k)) for k in range(n_dp - 1, 0, -1)]

    *state, order = pl.pallas_call(
        functools.partial(load_kernel, ranks, cols_a),
        in_specs=[HBM] * 9,
        out_specs=[VMEM] * 4 + [SMEM],
        out_shape=[pltpu.VMEM((ranks, cols), F32)] * 4 + [pltpu.SMEM((2,), jnp.int32)],
        scratch_shapes=[pltpu.SMEM(slot_of.shape, jnp.int32), pltpu.SemaphoreType.DMA((9,))],
        compiler_params=PARAMS,
        cost_estimate=estimate(4 * ranks * cols * 4),
        name="load",
    )(
        *map(
            left,
            (
                slot_of,
                grad_a,
                grad_b,
                factor_a,
                factor_b,
                moment_a,
                first_moment_factor_b,
                second_a,
                second_b,
            ),
        ),
    )
    state = [held(x) for x in state]

    send = pl.pallas_call(
        send_kernel,
        in_specs=[VMEM] * (3 + n_dp),
        out_specs=VMEM,
        out_shape=pltpu.VMEM((ranks, cols), BF16),
        compiler_params=PARAMS,
        name="send",
    )(*state, *got)

    def move(slots):
        pairs = [(expert, slot) for expert, slot in enumerate(slots) if expert != slot]

        def branch(send):
            mine = lax.ppermute(send, "expert", pairs) if pairs else send
            return pl.pallas_call(
                keep_kernel,
                in_specs=[VMEM],
                out_specs=VMEM,
                out_shape=pltpu.VMEM((ranks, cols), BF16),
                compiler_params=PARAMS,
                name="keep",
            )(held(mine))

        return branch

    if n_expert <= MOST_SWITCHED:
        orders = itertools.permutations(range(n_expert))
        mine = lax.switch(order[0], [move(slots) for slots in orders], send)
        mine = jnp.where(order[1] == 1, send, mine)
    else:
        mine = send
        here = lax.axis_index("expert")
        experts = jnp.arange(n_expert, dtype=jnp.int32)
        wanted = jnp.sum(jnp.where(slot_of == here, experts, 0)) ^ here
        for k in range(1, n_expert):
            mine = jnp.where(wanted == k, swap(send, "expert", n_expert, k), mine)

    parts = [mine] + [swap(mine, "dp", n_dp, k) for k in range(1, n_dp)]
    panel_shape = weight.shape[1:]
    shapes = [factor_a.shape, factor_b.shape] * 3
    *new, panel = pl.pallas_call(
        functools.partial(state_kernel, n_dp - 1, cols_a),
        in_specs=[HBM] + [VMEM] * (3 + n_dp),
        out_specs=[HBM] * 6 + [VMEM],
        out_shape=[jax.ShapeDtypeStruct(shape, F32) for shape in shapes]
        + [pltpu.VMEM(panel_shape, BF16)],
        scratch_shapes=[pltpu.VMEM(shape[1:], F32) for shape in shapes]
        + [pltpu.SemaphoreType.DMA((7,))],
        compiler_params=PARAMS,
        cost_estimate=estimate(weight.size * 4),
        name="state",
    )(left(weight), *state, *got)
    new_a, new_b, new_moment_a, new_moment_b, new_second_a, new_second_b = new
    rows_a, flipped, panel = pl.pallas_call(
        functools.partial(join_kernel, cols_a),
        in_specs=[VMEM] * (n_dp + 1),
        out_specs=[VMEM] * 3,
        out_shape=[
            pltpu.VMEM((ranks * n_dp, cols_a), BF16),
            pltpu.VMEM((cols_b, ranks * n_dp), BF16),
            pltpu.VMEM(panel_shape, BF16),
        ],
        input_output_aliases={n_dp: 2},
        compiler_params=PARAMS,
        name="join",
    )(*map(held, parts), held(panel))

    merged = None
    width = 512
    for k in range(n_tensor):
        block = held(rows_a if k == 0 else swap(rows_a, "tensor", n_tensor, k))
        operands = [held(panel), block, held(flipped)] + ([] if merged is None else [merged])
        merged = pl.pallas_call(
            functools.partial(merge_kernel, k, width),
            in_specs=[VMEM] * 3 + [HBM] * (len(operands) - 3),
            out_specs=HBM,
            out_shape=jax.ShapeDtypeStruct(weight.shape, BF16),
            scratch_shapes=[
                pltpu.VMEM((cols_a // width, panel_shape[0], width), BF16),
                pltpu.SemaphoreType.DMA((cols_a // width,)),
            ],
            input_output_aliases={} if merged is None else {3: 0},
            compiler_params=PARAMS,
            cost_estimate=estimate(
                panel_shape[0] * cols_a * 2, 2 * panel_shape[0] * cols_a * ranks * n_dp
            ),
            name=f"merge{k}",
        )(*operands)
    return (merged, new_a, new_b, new_moment_a, new_second_a, new_moment_b, new_second_b)


def solution(mesh):
    sizes = dict(mesh.shape)

    def body(*args):
        return per_device(sizes["dp"], sizes["expert"], sizes["tensor"], *args)

    state = P("expert", "dp", "tensor")
    grad = P("dp", "expert", None, "tensor")
    weight = P("expert", "tensor", None)
    in_specs = (weight,) + (state,) * 6 + (grad,) * 2 + (P(),)
    out_specs = (weight,) + (state,) * 6
    return jax.shard_map(body, mesh=mesh, in_specs=in_specs, out_specs=out_specs, check_vma=False)
```

profile of v0, /device:TPU:17, one launch (start us, length us, event | category | flops | bytes accessed | tf_op | source)
XLA Modules:
  0.0 28.3 jit_solution(2208170696910375329)
XLA Ops:
  0.6 1.2 %pack.1 = (bf16[16,2816]{1,0:T(8,128)(2,1)S(1)}, bf16[16,2816]{1,0:T(8,128)(2,1)S(1)}, bf16[16,2816]{1,0:T(8,128)(2,1)S(1)}) custom-call(f32[1,1,64,2048]{3,2,1,0:T(8,128)} %grad_a.1, f32[1,1,64,768]{3,2,1,0:T(8,128)} %grad_b.1), custom_call_target="tpu_custom_call" | custom-call | tf_op jit(solution)/shard_map/pack/pallas_call | solution.py:218
  1.8 2.2 %collective-permute-start.23 = (bf16[16,2816]{1,0:T(8,128)(2,1)S(1)}, bf16[16,2816]{1,0:T(8,128)(2,1)S(1)}, u32[]{:S(2)}, u32[]{:S(2)}) collective-permute-start(bf16[16,2816]{1,0:T(8,128)(2,1)S(1)} %get-tuple-element.79), channel_id=1, source_target_pairs={{0,24},{8,16},{16,8},{24,0},{1,25},{9,17},{17,9},{25,1},{2,26},{10... | collective-permute-start | bytes 270344 | tf_op jit(solution)/shard_map/ppermute | solution.py:42
  4.0 0.2 collective-permute-start.24
  4.3 0.3 collective-permute-start.25
  4.5 1.3 %load.1 = (f32[16,2816]{1,0:T(8,128)S(1)}, f32[16,2816]{1,0:T(8,128)S(1)}, f32[16,2816]{1,0:T(8,128)S(1)}, f32[16,2816]{1,0:T(8,128)S(1)}, s32[2]{0:T(128)S(4)}) custom-call(s32[4]{0:T(128)} %slots_in.1, f32[1,1,64,2048]{3,2,1,0:T(8,128)} %grad_a.1, f32[1,1,64,768]{3,2,1,0:T(8,128)} %grad_b.1, f32[1,16,2048]{2,1,0:T(8,128)} %refs_2_.1, ...), custom_call_target="tpu_custom_call" | custom-call | bytes 720896 | tf_op jit(solution)/shard_map/load/pallas_call | solution.py:232
  5.8 0.6 %fusion = (s32[1]{0:T(128)}, s32[1]{0:T(128)}) fusion(s32[2]{0:T(128)S(4)} %get-tuple-element.74), kind=kLoop, calls=%fused_computation.1 | loop fusion | bytes 16 | tf_op jit(solution)/shard_map/slice | solution.py:287
  7.7 0.0 collective-permute-done.23.refs_4_
  7.7 1.2 %collective-permute-done.24.refs_5_ = bf16[16,2816]{1,0:T(8,128)(2,1)S(1)} collective-permute-done((bf16[16,2816]{1,0:T(8,128)(2,1)S(1)}, bf16[16,2816]{1,0:T(8,128)(2,1)S(1)}, u32[]{:S(2)}, u32[]{:S(2)}) %collective-permute-start.24) | collective-permute-done | bytes 90144 | tf_op jit(solution)/shard_map/ppermute | solution.py:42
  8.9 0.0 collective-permute-done.25.refs_6_
  8.9 0.2 send.1
  9.0 5.3 %conditional.1 = (bf16[16,2816]{1,0:T(8,128)(2,1)S(1)}) conditional(s32[]{:T(128)} %bitcast.1, bf16[16,2816]{1,0:T(8,128)(2,1)S(1)} %send.1, bf16[16,2816]{1,0:T(8,128)(2,1)S(1)} %send.1, bf16[16,2816]{1,0:T(8,128)(2,1)S(1)} %send.1, bf16[16,2816]{1,0:T(8,128)(2,1)S(1)} %send.1, ...), branch_computations={%region_0.0_spmd, %region_1.0_spmd, %region_2.0_spmd, %region_3.0_... | conditional | bytes 360496 | solution.py:286
  9.1 2.1 %collective-permute-start.1 = (bf16[16,2816]{1,0:T(8,128)(2,1)S(1)}, bf16[16,2816]{1,0:T(8,128)(2,1)S(1)}, u32[]{:S(2)}, u32[]{:S(2)}) collective-permute-start(bf16[16,2816]{1,0:T(8,128)(2,1)S(1)} %param.2), channel_id=1, source_target_pairs={{2,4},{4,2},{3,5},{5,3},{10,12},{12,10},{11,13},{13,11},{18,20},{2... | collective-permute-start | bytes 270344 | tf_op jit(solution)/shard_map/cond/branch_2_fun/ppermute | solution.py:272
  11.2 3.2 %collective-permute-done.1.piece = bf16[16,2816]{1,0:T(8,128)(2,1)S(1)} collective-permute-done((bf16[16,2816]{1,0:T(8,128)(2,1)S(1)}, bf16[16,2816]{1,0:T(8,128)(2,1)S(1)}, u32[]{:S(2)}, u32[]{:S(2)}) %collective-permute-start.1) | collective-permute-done | bytes 90144 | tf_op jit(solution)/shard_map/cond/branch_2_fun/ppermute | solution.py:272
  14.4 1.1 %collective-permute-start.28 = (bf16[16,2816]{1,0:T(8,128)(2,1)S(1)}, bf16[16,2816]{1,0:T(8,128)(2,1)S(1)}, u32[]{:S(2)}, u32[]{:S(2)}) collective-permute-start(bf16[16,2816]{1,0:T(8,128)(2,1)S(1)} %broadcast_select_fusion.refs_0_), channel_id=1, source_target_pairs={{0,24},{8,16},{16,8},{24,0},{1,25},{9,17},{17,9},{25,1},{2,26},{10... | collective-permute-start | bytes 270344 | tf_op jit(solution)/shard_map/ppermute | solution.py:42
  15.5 1.5 %collective-permute-start.27 = (bf16[16,2816]{1,0:T(8,128)(2,1)S(1)}, bf16[16,2816]{1,0:T(8,128)(2,1)S(1)}, u32[]{:S(2)}, u32[]{:S(2)}) collective-permute-start(bf16[16,2816]{1,0:T(8,128)(2,1)S(1)} %broadcast_select_fusion.refs_0_), channel_id=1, source_target_pairs={{0,16},{8,24},{16,0},{24,8},{1,17},{9,25},{17,1},{25,9},{2,18},{10... | collective-permute-start | bytes 270344 | tf_op jit(solution)/shard_map/ppermute | solution.py:42
  17.0 0.1 collective-permute-start.26
  17.1 3.0 %state.1 = (f32[1,16,2048]{2,1,0:T(8,128)}, f32[1,16,768]{2,1,0:T(8,128)}, f32[1,16,2048]{2,1,0:T(8,128)}, f32[1,16,768]{2,1,0:T(8,128)}, f32[1,16,2048]{2,1,0:T...) custom-call(bf16[1,768,4096]{2,1,0:T(8,128)(2,1)} %weight.1, f32[16,2816]{1,0:T(8,128)S(1)} %get-tuple-element.75.refs_0_, ...), custom_call_target="tpu_custom_call" | custom-call | bytes 12582912 | tf_op jit(solution)/shard_map/state/pallas_call | solution.py:299
  20.2 0.0 collective-permute-done.28.refs_3_
  20.2 0.0 collective-permute-done.27.refs_2_
  20.2 0.2 collective-permute-done.26.refs_1_
  20.4 0.1 join.1
  20.5 3.7 %collective-permute-start.29 = (bf16[64,2048]{1,0:T(8,128)(2,1)S(1)}, bf16[64,2048]{1,0:T(8,128)(2,1)S(1)}, u32[]{:S(2)}, u32[]{:S(2)}) collective-permute-start(bf16[64,2048]{1,0:T(8,128)(2,1)S(1)} %get-tuple-element.84.refs_1_), channel_id=1, source_target_pairs={{0,1},{1,0},{2,3},{3,2},{4,5},{5,4},{6,7},{7,6},{8,9},{9,8},{10,11... | collective-permute-start | bytes 786440 | tf_op jit(solution)/shard_map/ppermute | solution.py:42
  24.2 2.0 %merge0.1.refs_3_ = bf16[1,768,4096]{2,1,0:T(8,128)(2,1)} custom-call(bf16[768,4096]{1,0:T(8,128)(2,1)S(1)} %get-tuple-element.83.refs_0_, bf16[64,2048]{1,0:T(8,128)(2,1)S(1)} %get-tuple-element.84.refs_1_, bf16[768,64]{1,0:T(8,128)(2,1)S(1)} %get-tuple-element.85.refs_2_), custom_call_target="tpu_custom_call" | custom-call | flops 201326592 | bytes 3145728 | tf_op jit(solution)/shard_map/merge0/pallas_call | solution.py:331
  26.3 0.0 collective-permute-done.29.refs_1_
  26.3 2.0 %merge1.1 = bf16[1,768,4096]{2,1,0:T(8,128)(2,1)} custom-call(bf16[768,4096]{1,0:T(8,128)(2,1)S(1)} %get-tuple-element.83.refs_0_, bf16[64,2048]{1,0:T(8,128)(2,1)S(1)} %collective-permute-done.29.refs_1_, bf16[768,64]{1,0:T(8,128)(2,1)S(1)} %get-tuple-element.85.refs_2_, bf16[1,768,4096]{2,1,0:T(8,128)(2,1)} %merge0.1.refs_3_), custom_call_target="tpu_custom_call", output_to_operand_aliasing={{}: (3, {})} | custom-call | flops 201326592 | bytes 3145728 | tf_op jit(solution)/shard_map/merge1/pallas_call | solution.py:331
  (2 shorter events, 0.0 us)
Async XLA Ops:
  1.8 5.9 %collective-permute-start.23 = (bf16[16,2816]{1,0:T(8,128)(2,1)S(1)}, bf16[16,2816]{1,0:T(8,128)(2,1)S(1)}, u32[]{:S(2)}, u32[]{:S(2)}) collective-permute-start(bf16[16,2816]{1,0:T(8,128)(2,1)S(1)} %get-tuple-element.79), channel_id=1, source_target_pairs={{0,24},{8,16},{16,8},{24,0},{1,25},{9,17},{17,9},{25,1},{2,26},{10... | collective-permute-start | bytes 270344 | tf_op jit(solution)/shard_map/ppermute | solution.py:42
  4.0 4.8 %collective-permute-start.24 = (bf16[16,2816]{1,0:T(8,128)(2,1)S(1)}, bf16[16,2816]{1,0:T(8,128)(2,1)S(1)}, u32[]{:S(2)}, u32[]{:S(2)}) collective-permute-start(bf16[16,2816]{1,0:T(8,128)(2,1)S(1)} %get-tuple-element.80), channel_id=1, source_target_pairs={{0,16},{8,24},{16,0},{24,8},{1,17},{9,25},{17,1},{25,9},{2,18},{10... | collective-permute-start | bytes 270344 | tf_op jit(solution)/shard_map/ppermute | solution.py:42
  4.3 4.6 %collective-permute-start.25 = (bf16[16,2816]{1,0:T(8,128)(2,1)S(1)}, bf16[16,2816]{1,0:T(8,128)(2,1)S(1)}, u32[]{:S(2)}, u32[]{:S(2)}) collective-permute-start(bf16[16,2816]{1,0:T(8,128)(2,1)S(1)} %get-tuple-element.81), channel_id=1, source_target_pairs={{0,8},{8,0},{16,24},{24,16},{1,9},{9,1},{17,25},{25,17},{2,10},{10... | collective-permute-start | bytes 270344 | tf_op jit(solution)/shard_map/ppermute | solution.py:42
  9.1 5.3 %collective-permute-start.1 = (bf16[16,2816]{1,0:T(8,128)(2,1)S(1)}, bf16[16,2816]{1,0:T(8,128)(2,1)S(1)}, u32[]{:S(2)}, u32[]{:S(2)}) collective-permute-start(bf16[16,2816]{1,0:T(8,128)(2,1)S(1)} %param.2), channel_id=1, source_target_pairs={{2,4},{4,2},{3,5},{5,3},{10,12},{12,10},{11,13},{13,11},{18,20},{2... | collective-permute-start | bytes 270344 | tf_op jit(solution)/shard_map/cond/branch_2_fun/ppermute | solution.py:272
  14.4 5.8 %collective-permute-start.28 = (bf16[16,2816]{1,0:T(8,128)(2,1)S(1)}, bf16[16,2816]{1,0:T(8,128)(2,1)S(1)}, u32[]{:S(2)}, u32[]{:S(2)}) collective-permute-start(bf16[16,2816]{1,0:T(8,128)(2,1)S(1)} %broadcast_select_fusion.refs_0_), channel_id=1, source_target_pairs={{0,24},{8,16},{16,8},{24,0},{1,25},{9,17},{17,9},{25,1},{2,26},{10... | collective-permute-start | bytes 270344 | tf_op jit(solution)/shard_map/ppermute | solution.py:42
  15.5 4.7 %collective-permute-start.27 = (bf16[16,2816]{1,0:T(8,128)(2,1)S(1)}, bf16[16,2816]{1,0:T(8,128)(2,1)S(1)}, u32[]{:S(2)}, u32[]{:S(2)}) collective-permute-start(bf16[16,2816]{1,0:T(8,128)(2,1)S(1)} %broadcast_select_fusion.refs_0_), channel_id=1, source_target_pairs={{0,16},{8,24},{16,0},{24,8},{1,17},{9,25},{17,1},{25,9},{2,18},{10... | collective-permute-start | bytes 270344 | tf_op jit(solution)/shard_map/ppermute | solution.py:42
  17.0 3.4 %collective-permute-start.26 = (bf16[16,2816]{1,0:T(8,128)(2,1)S(1)}, bf16[16,2816]{1,0:T(8,128)(2,1)S(1)}, u32[]{:S(2)}, u32[]{:S(2)}) collective-permute-start(bf16[16,2816]{1,0:T(8,128)(2,1)S(1)} %broadcast_select_fusion.refs_0_), channel_id=1, source_target_pairs={{0,8},{8,0},{16,24},{24,16},{1,9},{9,1},{17,25},{25,17},{2,10},{10... | collective-permute-start | bytes 270344 | tf_op jit(solution)/shard_map/ppermute | solution.py:42
  20.5 5.7 %collective-permute-start.29 = (bf16[64,2048]{1,0:T(8,128)(2,1)S(1)}, bf16[64,2048]{1,0:T(8,128)(2,1)S(1)}, u32[]{:S(2)}, u32[]{:S(2)}) collective-permute-start(bf16[64,2048]{1,0:T(8,128)(2,1)S(1)} %get-tuple-element.84.refs_1_), channel_id=1, source_target_pairs={{0,1},{1,0},{2,3},{3,2},{4,5},{5,4},{6,7},{7,6},{8,9},{9,8},{10,11... | collective-permute-start | bytes 786440 | tf_op jit(solution)/shard_map/ppermute | solution.py:42
where the time goes:
time: 28.5 us; the launch traced here: 28.3 us
  starting transfers between devices  11.2 us (39%)
  Pallas kernels  9.84 us (35%)
  waiting for transfers between devices  4.56 us (16%)
  between operations  2.02 us (7%)
  local copies, waits for them, and re-layouts  0.6 us (2%)
    ppermute x7, starting transfers between devices, swap(): return lax.ppermute(x, axis, [(i, i ^ k) for i in range(n)])  9.13 us
    pallas_call x2, Pallas kernels, per_device(): pl.pallas_call(functools.partial(merge_kernel, k, width), in_specs=[VMEM]...  4.06 us
    ppermute x1, waiting for transfers between devices, branch(): mine = lax.ppermute(send, 'expert', pairs) if pairs else send  3.19 us
    pallas_call x1, Pallas kernels, per_device(): pl.pallas_call(functools.partial(state_kernel, n_dp - 1, cols_a), in_spec...  3.04 us
    ppermute x1, starting transfers between devices, branch(): mine = lax.ppermute(send, 'expert', pairs) if pairs else send  2.08 us
    ppermute x7, waiting for transfers between devices, swap(): return lax.ppermute(x, axis, [(i, i ^ k) for i in range(n)])  1.37 us
    pallas_call x1, Pallas kernels, per_device(): pl.pallas_call(functools.partial(load_kernel, ranks, cols_a), in_specs=[H...  1.25 us
    pallas_call x1, Pallas kernels, per_device(): pl.pallas_call(functools.partial(pack_kernel, n_dp, ranks, cols_a), in_sp...  1.16 us
  transfers between devices with their start and end apart: 8, of which 3 were waited for; matrix products, arithmetic and copies ran while one was open for 2% of the time, Pallas kernels for 22%

commit v1 on v0

--- a/solution.py
+++ b/solution.py
@@ -266,10 +266,15 @@
     )(*state, *got)
 
     def move(slots):
-        pairs = [(expert, slot) for expert, slot in enumerate(slots) if expert != slot]
+        pairs = [
+            (i * n_expert + expert, (i if expert != slot else i ^ 1) * n_expert + slot)
+            for i in range(n_dp)
+            for expert, slot in enumerate(slots)
+        ]
+        moves = any(expert != slot for expert, slot in enumerate(slots))
 
         def branch(send):
-            mine = lax.ppermute(send, "expert", pairs) if pairs else send
+            mine = lax.ppermute(send, ("dp", "expert"), pairs) if moves else send
             return pl.pallas_call(
                 keep_kernel,
                 in_specs=[VMEM],

time: 28.5 us -> 29.1 us (1.021)
  the two profiles are of different devices: /device:TPU:17 before, /device:TPU:1 now
where the time goes in v1:
time: 29.1 us; the launch traced here: 29.2 us
  starting transfers between devices  13.4 us (46%)
  Pallas kernels  9.84 us (34%)
  waiting for transfers between devices  3.25 us (11%)
  between operations  2.02 us (7%)
  local copies, waits for them, and re-layouts  0.6 us (2%)
    ppermute x7, starting transfers between devices, swap(): return lax.ppermute(x, axis, [(i, i ^ k) for i in range(n)])  9.73 us
    pallas_call x2, Pallas kernels, per_device(): pl.pallas_call(functools.partial(merge_kernel, k, width), in_specs=[VMEM]...  4.06 us
    ppermute x1, starting transfers between devices, branch(): mine = lax.ppermute(send, ('dp', 'expert'), pairs) if moves else send  3.66 us
    pallas_call x1, Pallas kernels, per_device(): pl.pallas_call(functools.partial(state_kernel, n_dp - 1, cols_a), in_spec...  3.04 us
    ppermute x1, waiting for transfers between devices, branch(): mine = lax.ppermute(send, ('dp', 'expert'), pairs) if moves else send  2.02 us
    pallas_call x1, Pallas kernels, per_device(): pl.pallas_call(functools.partial(load_kernel, ranks, cols_a), in_specs=[H...  1.25 us
    ppermute x7, waiting for transfers between devices, swap(): return lax.ppermute(x, axis, [(i, i ^ k) for i in range(n)])  1.22 us
    pallas_call x1, Pallas kernels, per_device(): pl.pallas_call(functools.partial(pack_kernel, n_dp, ranks, cols_a), in_sp...  1.16 us
  transfers between devices with their start and end apart: 8, of which 4 were waited for; matrix products, arithmetic and copies ran while one was open for 2% of the time, Pallas kernels for 22%

profile of v1, /device:TPU:1, one launch (start us, length us, event | category | flops | bytes accessed | tf_op | source)
XLA Modules:
  0.0 29.2 jit_solution(17892820547222899717)
XLA Ops:
  0.6 1.2 %pack.1 = (bf16[16,2816]{1,0:T(8,128)(2,1)S(1)}, bf16[16,2816]{1,0:T(8,128)(2,1)S(1)}, bf16[16,2816]{1,0:T(8,128)(2,1)S(1)}) custom-call(f32[1,1,64,2048]{3,2,1,0:T(8,128)} %grad_a.1, f32[1,1,64,768]{3,2,1,0:T(8,128)} %grad_b.1), custom_call_target="tpu_custom_call" | custom-call | tf_op jit(solution)/shard_map/pack/pallas_call | solution.py:218
  1.8 3.1 %collective-permute-start.23 = (bf16[16,2816]{1,0:T(8,128)(2,1)S(1)}, bf16[16,2816]{1,0:T(8,128)(2,1)S(1)}, u32[]{:S(2)}, u32[]{:S(2)}) collective-permute-start(bf16[16,2816]{1,0:T(8,128)(2,1)S(1)} %get-tuple-element.79), channel_id=1, source_target_pairs={{0,24},{8,16},{16,8},{24,0},{1,25},{9,17},{17,9},{25,1},{2,26},{10... | collective-permute-start | bytes 270344 | tf_op jit(solution)/shard_map/ppermute | solution.py:42
  4.9 0.2 collective-permute-start.24
  5.1 0.1 collective-permute-start.25
  5.2 1.3 %load.1 = (f32[16,2816]{1,0:T(8,128)S(1)}, f32[16,2816]{1,0:T(8,128)S(1)}, f32[16,2816]{1,0:T(8,128)S(1)}, f32[16,2816]{1,0:T(8,128)S(1)}, s32[2]{0:T(128)S(4)}) custom-call(s32[4]{0:T(128)} %slots_in.1, f32[1,1,64,2048]{3,2,1,0:T(8,128)} %grad_a.1, f32[1,1,64,768]{3,2,1,0:T(8,128)} %grad_b.1, f32[1,16,2048]{2,1,0:T(8,128)} %refs_2_.1, ...), custom_call_target="tpu_custom_call" | custom-call | bytes 720896 | tf_op jit(solution)/shard_map/load/pallas_call | solution.py:232
  6.5 0.6 %fusion = (s32[1]{0:T(128)}, s32[1]{0:T(128)}) fusion(s32[2]{0:T(128)S(4)} %get-tuple-element.74), kind=kLoop, calls=%fused_computation.1 | loop fusion | bytes 16 | tf_op jit(solution)/shard_map/slice | solution.py:292
  8.4 0.0 collective-permute-done.23.refs_4_
  8.4 0.5 %collective-permute-done.24.refs_5_ = bf16[16,2816]{1,0:T(8,128)(2,1)S(1)} collective-permute-done((bf16[16,2816]{1,0:T(8,128)(2,1)S(1)}, bf16[16,2816]{1,0:T(8,128)(2,1)S(1)}, u32[]{:S(2)}, u32[]{:S(2)}) %collective-permute-start.24) | collective-permute-done | bytes 90144 | tf_op jit(solution)/shard_map/ppermute | solution.py:42
  8.9 0.5 %collective-permute-done.25.refs_6_ = bf16[16,2816]{1,0:T(8,128)(2,1)S(1)} collective-permute-done((bf16[16,2816]{1,0:T(8,128)(2,1)S(1)}, bf16[16,2816]{1,0:T(8,128)(2,1)S(1)}, u32[]{:S(2)}, u32[]{:S(2)}) %collective-permute-start.25) | collective-permute-done | bytes 90144 | tf_op jit(solution)/shard_map/ppermute | solution.py:42
  9.4 0.2 send.1
  9.6 5.8 %conditional.1 = (bf16[16,2816]{1,0:T(8,128)(2,1)S(1)}) conditional(s32[]{:T(128)} %bitcast.1, bf16[16,2816]{1,0:T(8,128)(2,1)S(1)} %send.1, bf16[16,2816]{1,0:T(8,128)(2,1)S(1)} %send.1, bf16[16,2816]{1,0:T(8,128)(2,1)S(1)} %send.1, bf16[16,2816]{1,0:T(8,128)(2,1)S(1)} %send.1, ...), branch_computations={%region_0.0_spmd, %region_1.0_spmd, %region_2.0_spmd, %region_3.0_... | conditional | bytes 360496 | solution.py:291
  9.7 3.7 %collective-permute-start.22 = (bf16[16,2816]{1,0:T(8,128)(2,1)S(1)}, bf16[16,2816]{1,0:T(8,128)(2,1)S(1)}, u32[]{:S(2)}, u32[]{:S(2)}) collective-permute-start(bf16[16,2816]{1,0:T(8,128)(2,1)S(1)} %param.23), channel_id=1, source_target_pairs={{0,6},{2,4},{4,2},{6,0},{8,14},{10,12},{12,10},{14,8},{16,22},{18,... | collective-permute-start | bytes 270344 | tf_op jit(solution)/shard_map/cond/branch_23_fun/ppermute | solution.py:277
  13.3 2.0 %collective-permute-done.22.piece = bf16[16,2816]{1,0:T(8,128)(2,1)S(1)} collective-permute-done((bf16[16,2816]{1,0:T(8,128)(2,1)S(1)}, bf16[16,2816]{1,0:T(8,128)(2,1)S(1)}, u32[]{:S(2)}, u32[]{:S(2)}) %collective-permute-start.22) | collective-permute-done | bytes 90144 | tf_op jit(solution)/shard_map/cond/branch_23_fun/ppermute | solution.py:277
  15.4 1.1 %collective-permute-start.28 = (bf16[16,2816]{1,0:T(8,128)(2,1)S(1)}, bf16[16,2816]{1,0:T(8,128)(2,1)S(1)}, u32[]{:S(2)}, u32[]{:S(2)}) collective-permute-start(bf16[16,2816]{1,0:T(8,128)(2,1)S(1)} %broadcast_select_fusion.refs_0_), channel_id=1, source_target_pairs={{0,24},{8,16},{16,8},{24,0},{1,25},{9,17},{17,9},{25,1},{2,26},{10... | collective-permute-start | bytes 270344 | tf_op jit(solution)/shard_map/ppermute | solution.py:42
  16.5 1.5 %collective-permute-start.27 = (bf16[16,2816]{1,0:T(8,128)(2,1)S(1)}, bf16[16,2816]{1,0:T(8,128)(2,1)S(1)}, u32[]{:S(2)}, u32[]{:S(2)}) collective-permute-start(bf16[16,2816]{1,0:T(8,128)(2,1)S(1)} %broadcast_select_fusion.refs_0_), channel_id=1, source_target_pairs={{0,16},{8,24},{16,0},{24,8},{1,17},{9,25},{17,1},{25,9},{2,18},{10... | collective-permute-start | bytes 270344 | tf_op jit(solution)/shard_map/ppermute | solution.py:42
  18.0 0.1 collective-permute-start.26
  18.1 3.0 %state.1 = (f32[1,16,2048]{2,1,0:T(8,128)}, f32[1,16,768]{2,1,0:T(8,128)}, f32[1,16,2048]{2,1,0:T(8,128)}, f32[1,16,768]{2,1,0:T(8,128)}, f32[1,16,2048]{2,1,0:T...) custom-call(bf16[1,768,4096]{2,1,0:T(8,128)(2,1)} %weight.1, f32[16,2816]{1,0:T(8,128)S(1)} %get-tuple-element.75.refs_0_, ...), custom_call_target="tpu_custom_call" | custom-call | bytes 12582912 | tf_op jit(solution)/shard_map/state/pallas_call | solution.py:304
  21.2 0.0 collective-permute-done.28.refs_3_
  21.2 0.0 collective-permute-done.27.refs_2_
  21.2 0.2 collective-permute-done.26.refs_1_
  21.4 0.1 join.1
  21.5 3.6 %collective-permute-start.29 = (bf16[64,2048]{1,0:T(8,128)(2,1)S(1)}, bf16[64,2048]{1,0:T(8,128)(2,1)S(1)}, u32[]{:S(2)}, u32[]{:S(2)}) collective-permute-start(bf16[64,2048]{1,0:T(8,128)(2,1)S(1)} %get-tuple-element.84.refs_1_), channel_id=1, source_target_pairs={{0,1},{1,0},{2,3},{3,2},{4,5},{5,4},{6,7},{7,6},{8,9},{9,8},{10,11... | collective-permute-start | bytes 786440 | tf_op jit(solution)/shard_map/ppermute | solution.py:42
  25.1 2.0 %merge0.1.refs_3_ = bf16[1,768,4096]{2,1,0:T(8,128)(2,1)} custom-call(bf16[768,4096]{1,0:T(8,128)(2,1)S(1)} %get-tuple-element.83.refs_0_, bf16[64,2048]{1,0:T(8,128)(2,1)S(1)} %get-tuple-element.84.refs_1_, bf16[768,64]{1,0:T(8,128)(2,1)S(1)} %get-tuple-element.85.refs_2_), custom_call_target="tpu_custom_call" | custom-call | flops 201326592 | bytes 3145728 | tf_op jit(solution)/shard_map/merge0/pallas_call | solution.py:336
  27.1 0.0 collective-permute-done.29.refs_1_
  27.2 2.0 %merge1.1 = bf16[1,768,4096]{2,1,0:T(8,128)(2,1)} custom-call(bf16[768,4096]{1,0:T(8,128)(2,1)S(1)} %get-tuple-element.83.refs_0_, bf16[64,2048]{1,0:T(8,128)(2,1)S(1)} %collective-permute-done.29.refs_1_, bf16[768,64]{1,0:T(8,128)(2,1)S(1)} %get-tuple-element.85.refs_2_, bf16[1,768,4096]{2,1,0:T(8,128)(2,1)} %merge0.1.refs_3_), custom_call_target="tpu_custom_call", output_to_operand_aliasing={{}: (3, {})} | custom-call | flops 201326592 | bytes 3145728 | tf_op jit(solution)/shard_map/merge1/pallas_call | solution.py:336
  (2 shorter events, 0.0 us)
Async XLA Ops:
  1.8 6.6 %collective-permute-start.23 = (bf16[16,2816]{1,0:T(8,128)(2,1)S(1)}, bf16[16,2816]{1,0:T(8,128)(2,1)S(1)}, u32[]{:S(2)}, u32[]{:S(2)}) collective-permute-start(bf16[16,2816]{1,0:T(8,128)(2,1)S(1)} %get-tuple-element.79), channel_id=1, source_target_pairs={{0,24},{8,16},{16,8},{24,0},{1,25},{9,17},{17,9},{25,1},{2,26},{10... | collective-permute-start | bytes 270344 | tf_op jit(solution)/shard_map/ppermute | solution.py:42
  4.9 4.1 %collective-permute-start.24 = (bf16[16,2816]{1,0:T(8,128)(2,1)S(1)}, bf16[16,2816]{1,0:T(8,128)(2,1)S(1)}, u32[]{:S(2)}, u32[]{:S(2)}) collective-permute-start(bf16[16,2816]{1,0:T(8,128)(2,1)S(1)} %get-tuple-element.80), channel_id=1, source_target_pairs={{0,16},{8,24},{16,0},{24,8},{1,17},{9,25},{17,1},{25,9},{2,18},{10... | collective-permute-start | bytes 270344 | tf_op jit(solution)/shard_map/ppermute | solution.py:42
  5.1 4.3 %collective-permute-start.25 = (bf16[16,2816]{1,0:T(8,128)(2,1)S(1)}, bf16[16,2816]{1,0:T(8,128)(2,1)S(1)}, u32[]{:S(2)}, u32[]{:S(2)}) collective-permute-start(bf16[16,2816]{1,0:T(8,128)(2,1)S(1)} %get-tuple-element.81), channel_id=1, source_target_pairs={{0,8},{8,0},{16,24},{24,16},{1,9},{9,1},{17,25},{25,17},{2,10},{10... | collective-permute-start | bytes 270344 | tf_op jit(solution)/shard_map/ppermute | solution.py:42
  9.7 5.7 %collective-permute-start.22 = (bf16[16,2816]{1,0:T(8,128)(2,1)S(1)}, bf16[16,2816]{1,0:T(8,128)(2,1)S(1)}, u32[]{:S(2)}, u32[]{:S(2)}) collective-permute-start(bf16[16,2816]{1,0:T(8,128)(2,1)S(1)} %param.23), channel_id=1, source_target_pairs={{0,6},{2,4},{4,2},{6,0},{8,14},{10,12},{12,10},{14,8},{16,22},{18,... | collective-permute-start | bytes 270344 | tf_op jit(solution)/shard_map/cond/branch_23_fun/ppermute | solution.py:277
  15.4 5.8 %collective-permute-start.28 = (bf16[16,2816]{1,0:T(8,128)(2,1)S(1)}, bf16[16,2816]{1,0:T(8,128)(2,1)S(1)}, u32[]{:S(2)}, u32[]{:S(2)}) collective-permute-start(bf16[16,2816]{1,0:T(8,128)(2,1)S(1)} %broadcast_select_fusion.refs_0_), channel_id=1, source_target_pairs={{0,24},{8,16},{16,8},{24,0},{1,25},{9,17},{17,9},{25,1},{2,26},{10... | collective-permute-start | bytes 270344 | tf_op jit(solution)/shard_map/ppermute | solution.py:42
  16.5 4.7 %collective-permute-start.27 = (bf16[16,2816]{1,0:T(8,128)(2,1)S(1)}, bf16[16,2816]{1,0:T(8,128)(2,1)S(1)}, u32[]{:S(2)}, u32[]{:S(2)}) collective-permute-start(bf16[16,2816]{1,0:T(8,128)(2,1)S(1)} %broadcast_select_fusion.refs_0_), channel_id=1, source_target_pairs={{0,16},{8,24},{16,0},{24,8},{1,17},{9,25},{17,1},{25,9},{2,18},{10... | collective-permute-start | bytes 270344 | tf_op jit(solution)/shard_map/ppermute | solution.py:42
  18.0 3.4 %collective-permute-start.26 = (bf16[16,2816]{1,0:T(8,128)(2,1)S(1)}, bf16[16,2816]{1,0:T(8,128)(2,1)S(1)}, u32[]{:S(2)}, u32[]{:S(2)}) collective-permute-start(bf16[16,2816]{1,0:T(8,128)(2,1)S(1)} %broadcast_select_fusion.refs_0_), channel_id=1, source_target_pairs={{0,8},{8,0},{16,24},{24,16},{1,9},{9,1},{17,25},{25,17},{2,10},{10... | collective-permute-start | bytes 270344 | tf_op jit(solution)/shard_map/ppermute | solution.py:42
  21.5 5.6 %collective-permute-start.29 = (bf16[64,2048]{1,0:T(8,128)(2,1)S(1)}, bf16[64,2048]{1,0:T(8,128)(2,1)S(1)}, u32[]{:S(2)}, u32[]{:S(2)}) collective-permute-start(bf16[64,2048]{1,0:T(8,128)(2,1)S(1)} %get-tuple-element.84.refs_1_), channel_id=1, source_target_pairs={{0,1},{1,0},{2,3},{3,2},{4,5},{5,4},{6,7},{7,6},{8,9},{9,8},{10,11... | collective-permute-start | bytes 786440 | tf_op jit(solution)/shard_map/ppermute | solution.py:42

commit v2 on v1

--- a/solution.py
+++ b/solution.py
@@ -227,7 +227,8 @@
         compiler_params=PARAMS,
         name="pack",
     )(left(grad_a), left(grad_b))
-    got = [held(swap(pieces[k - 1], "dp", n_dp, k)) for k in range(n_dp - 1, 0, -1)]
+    ks = sorted(range(1, n_dp), key=lambda k: (-bin(k).count("1"), k))
+    got = [held(swap(pieces[k - 1], "dp", n_dp, k)) for k in ks]
 
     *state, order = pl.pallas_call(
         functools.partial(load_kernel, ranks, cols_a),
@@ -298,7 +299,7 @@
         for k in range(1, n_expert):
             mine = jnp.where(wanted == k, swap(send, "expert", n_expert, k), mine)
 
-    parts = [mine] + [swap(mine, "dp", n_dp, k) for k in range(1, n_dp)]
+    parts = [mine] + [swap(mine, "dp", n_dp, k) for k in ks[::-1]]
     panel_shape = weight.shape[1:]
     shapes = [factor_a.shape, factor_b.shape] * 3
     *new, panel = pl.pallas_call(

time: 29.1 us -> 29.3 us (level); the launches traced: 29.2 us -> 29.1 us
  starting transfers between devices: 13.4 us -> 11.4 us
  waiting for transfers between devices: 3.25 us -> 5.18 us
    ppermute x1, starting transfers between devices: 3.66 us -> 1.37 us  [branch(): mine = lax.ppermute(send, ('dp', 'expert'), pairs) if moves else send]
    ppermute x1, waiting for transfers between devices: 2.02 us -> 3.94 us  [branch(): mine = lax.ppermute(send, ('dp', 'expert'), pairs) if moves else send]
  transfers between devices with their start and end apart: 8 -> 8, of which waited for: 4 -> 3; matrix products, arithmetic and copies ran while one was open for 2% -> 2% of each run, Pallas kernels for 22% -> 22%
where the time goes in v2:
time: 29.3 us; the launch traced here: 29.1 us
  starting transfers between devices  11.4 us (39%)
  Pallas kernels  9.84 us (34%)
  waiting for transfers between devices  5.18 us (18%)
  between operations  2.02 us (7%)
  local copies, waits for them, and re-layouts  0.6 us (2%)
    ppermute x7, starting transfers between devices, swap(): return lax.ppermute(x, axis, [(i, i ^ k) for i in range(n)])  9.98 us
    pallas_call x2, Pallas kernels, per_device(): pl.pallas_call(functools.partial(merge_kernel, k, width), in_specs=[VMEM]...  4.06 us
    ppermute x1, waiting for transfers between devices, branch(): mine = lax.ppermute(send, ('dp', 'expert'), pairs) if moves else send  3.94 us
    pallas_call x1, Pallas kernels, per_device(): pl.pallas_call(functools.partial(state_kernel, n_dp - 1, cols_a), in_spec...  3.04 us
    ppermute x1, starting transfers between devices, branch(): mine = lax.ppermute(send, ('dp', 'expert'), pairs) if moves else send  1.37 us
    pallas_call x1, Pallas kernels, per_device(): pl.pallas_call(functools.partial(load_kernel, ranks, cols_a), in_specs=[H...  1.25 us
    ppermute x7, waiting for transfers between devices, swap(): return lax.ppermute(x, axis, [(i, i ^ k) for i in range(n)])  1.24 us
    pallas_call x1, Pallas kernels, per_device(): pl.pallas_call(functools.partial(pack_kernel, n_dp, ranks, cols_a), in_sp...  1.16 us
  transfers between devices with their start and end apart: 8, of which 3 were waited for; matrix products, arithmetic and copies ran while one was open for 2% of the time, Pallas kernels for 22%

profile of v2, /device:TPU:1, one launch (start us, length us, event | category | flops | bytes accessed | tf_op | source)
XLA Modules:
  0.0 29.1 jit_solution(6654824756560191235)
XLA Ops:
  0.6 1.2 %pack.1 = (bf16[16,2816]{1,0:T(8,128)(2,1)S(1)}, bf16[16,2816]{1,0:T(8,128)(2,1)S(1)}, bf16[16,2816]{1,0:T(8,128)(2,1)S(1)}) custom-call(f32[1,1,64,2048]{3,2,1,0:T(8,128)} %grad_a.1, f32[1,1,64,768]{3,2,1,0:T(8,128)} %grad_b.1), custom_call_target="tpu_custom_call" | custom-call | tf_op jit(solution)/shard_map/pack/pallas_call | solution.py:218
  1.8 3.1 %collective-permute-start.23 = (bf16[16,2816]{1,0:T(8,128)(2,1)S(1)}, bf16[16,2816]{1,0:T(8,128)(2,1)S(1)}, u32[]{:S(2)}, u32[]{:S(2)}) collective-permute-start(bf16[16,2816]{1,0:T(8,128)(2,1)S(1)} %get-tuple-element.79), channel_id=1, source_target_pairs={{0,24},{8,16},{16,8},{24,0},{1,25},{9,17},{17,9},{25,1},{2,26},{10... | collective-permute-start | bytes 270344 | tf_op jit(solution)/shard_map/ppermute | solution.py:42
  4.9 0.3 collective-permute-start.24
  5.1 0.1 collective-permute-start.25
  5.2 1.3 %load.1 = (f32[16,2816]{1,0:T(8,128)S(1)}, f32[16,2816]{1,0:T(8,128)S(1)}, f32[16,2816]{1,0:T(8,128)S(1)}, f32[16,2816]{1,0:T(8,128)S(1)}, s32[2]{0:T(128)S(4)}) custom-call(s32[4]{0:T(128)} %slots_in.1, f32[1,1,64,2048]{3,2,1,0:T(8,128)} %grad_a.1, f32[1,1,64,768]{3,2,1,0:T(8,128)} %grad_b.1, f32[1,16,2048]{2,1,0:T(8,128)} %refs_2_.1, ...), custom_call_target="tpu_custom_call" | custom-call | bytes 720896 | tf_op jit(solution)/shard_map/load/pallas_call | solution.py:233
  6.5 0.6 %fusion = (s32[1]{0:T(128)}, s32[1]{0:T(128)}) fusion(s32[2]{0:T(128)S(4)} %get-tuple-element.74), kind=kLoop, calls=%fused_computation.1 | loop fusion | bytes 16 | tf_op jit(solution)/shard_map/slice | solution.py:293
  8.4 0.0 collective-permute-done.23.refs_4_
  8.4 1.1 %collective-permute-done.24.refs_5_ = bf16[16,2816]{1,0:T(8,128)(2,1)S(1)} collective-permute-done((bf16[16,2816]{1,0:T(8,128)(2,1)S(1)}, bf16[16,2816]{1,0:T(8,128)(2,1)S(1)}, u32[]{:S(2)}, u32[]{:S(2)}) %collective-permute-start.24) | collective-permute-done | bytes 90144 | tf_op jit(solution)/shard_map/ppermute | solution.py:42
  9.5 0.0 collective-permute-done.25.refs_6_
  9.5 0.2 send.1
  9.7 5.4 %conditional.1 = (bf16[16,2816]{1,0:T(8,128)(2,1)S(1)}) conditional(s32[]{:T(128)} %bitcast.1, bf16[16,2816]{1,0:T(8,128)(2,1)S(1)} %send.1, bf16[16,2816]{1,0:T(8,128)(2,1)S(1)} %send.1, bf16[16,2816]{1,0:T(8,128)(2,1)S(1)} %send.1, bf16[16,2816]{1,0:T(8,128)(2,1)S(1)} %send.1, ...), branch_computations={%region_0.0_spmd, %region_1.0_spmd, %region_2.0_spmd, %region_3.0_... | conditional | bytes 360496 | solution.py:292
  9.7 1.4 %collective-permute-start.10 = (bf16[16,2816]{1,0:T(8,128)(2,1)S(1)}, bf16[16,2816]{1,0:T(8,128)(2,1)S(1)}, u32[]{:S(2)}, u32[]{:S(2)}) collective-permute-start(bf16[16,2816]{1,0:T(8,128)(2,1)S(1)} %param.11), channel_id=1, source_target_pairs={{0,2},{2,6},{4,12},{6,0},{8,10},{10,14},{12,4},{14,8},{16,18},{18,... | collective-permute-start | bytes 270344 | tf_op jit(solution)/shard_map/cond/branch_11_fun/ppermute | solution.py:278
  11.1 3.9 %collective-permute-done.10.piece = bf16[16,2816]{1,0:T(8,128)(2,1)S(1)} collective-permute-done((bf16[16,2816]{1,0:T(8,128)(2,1)S(1)}, bf16[16,2816]{1,0:T(8,128)(2,1)S(1)}, u32[]{:S(2)}, u32[]{:S(2)}) %collective-permute-start.10) | collective-permute-done | bytes 90144 | tf_op jit(solution)/shard_map/cond/branch_11_fun/ppermute | solution.py:278
  15.1 2.1 %collective-permute-start.28 = (bf16[16,2816]{1,0:T(8,128)(2,1)S(1)}, bf16[16,2816]{1,0:T(8,128)(2,1)S(1)}, u32[]{:S(2)}, u32[]{:S(2)}) collective-permute-start(bf16[16,2816]{1,0:T(8,128)(2,1)S(1)} %broadcast_select_fusion.refs_0_), channel_id=1, source_target_pairs={{0,24},{8,16},{16,8},{24,0},{1,25},{9,17},{17,9},{25,1},{2,26},{10... | collective-permute-start | bytes 270344 | tf_op jit(solution)/shard_map/ppermute | solution.py:42
  17.2 0.4 %collective-permute-start.27 = (bf16[16,2816]{1,0:T(8,128)(2,1)S(1)}, bf16[16,2816]{1,0:T(8,128)(2,1)S(1)}, u32[]{:S(2)}, u32[]{:S(2)}) collective-permute-start(bf16[16,2816]{1,0:T(8,128)(2,1)S(1)} %broadcast_select_fusion.refs_0_), channel_id=1, source_target_pairs={{0,8},{8,0},{16,24},{24,16},{1,9},{9,1},{17,25},{25,17},{2,10},{10... | collective-permute-start | bytes 270344 | tf_op jit(solution)/shard_map/ppermute | solution.py:42
  17.6 0.2 collective-permute-start.26
  17.8 3.0 %state.1 = (f32[1,16,2048]{2,1,0:T(8,128)}, f32[1,16,768]{2,1,0:T(8,128)}, f32[1,16,2048]{2,1,0:T(8,128)}, f32[1,16,768]{2,1,0:T(8,128)}, f32[1,16,2048]{2,1,0:T...) custom-call(bf16[1,768,4096]{2,1,0:T(8,128)(2,1)} %weight.1, f32[16,2816]{1,0:T(8,128)S(1)} %get-tuple-element.75.refs_0_, ...), custom_call_target="tpu_custom_call" | custom-call | bytes 12582912 | tf_op jit(solution)/shard_map/state/pallas_call | solution.py:305
  20.8 0.0 collective-permute-done.28.refs_3_
  20.9 0.0 collective-permute-done.27.refs_2_
  20.9 0.1 collective-permute-done.26.refs_1_
  21.0 0.1 join.1
  21.1 3.8 %collective-permute-start.29 = (bf16[64,2048]{1,0:T(8,128)(2,1)S(1)}, bf16[64,2048]{1,0:T(8,128)(2,1)S(1)}, u32[]{:S(2)}, u32[]{:S(2)}) collective-permute-start(bf16[64,2048]{1,0:T(8,128)(2,1)S(1)} %get-tuple-element.84.refs_1_), channel_id=1, source_target_pairs={{0,1},{1,0},{2,3},{3,2},{4,5},{5,4},{6,7},{7,6},{8,9},{9,8},{10,11... | collective-permute-start | bytes 786440 | tf_op jit(solution)/shard_map/ppermute | solution.py:42
  25.0 2.0 %merge0.1.refs_3_ = bf16[1,768,4096]{2,1,0:T(8,128)(2,1)} custom-call(bf16[768,4096]{1,0:T(8,128)(2,1)S(1)} %get-tuple-element.83.refs_0_, bf16[64,2048]{1,0:T(8,128)(2,1)S(1)} %get-tuple-element.84.refs_1_, bf16[768,64]{1,0:T(8,128)(2,1)S(1)} %get-tuple-element.85.refs_2_), custom_call_target="tpu_custom_call" | custom-call | flops 201326592 | bytes 3145728 | tf_op jit(solution)/shard_map/merge0/pallas_call | solution.py:337
  27.0 0.0 collective-permute-done.29.refs_1_
  27.0 2.0 %merge1.1 = bf16[1,768,4096]{2,1,0:T(8,128)(2,1)} custom-call(bf16[768,4096]{1,0:T(8,128)(2,1)S(1)} %get-tuple-element.83.refs_0_, bf16[64,2048]{1,0:T(8,128)(2,1)S(1)} %collective-permute-done.29.refs_1_, bf16[768,64]{1,0:T(8,128)(2,1)S(1)} %get-tuple-element.85.refs_2_, bf16[1,768,4096]{2,1,0:T(8,128)(2,1)} %merge0.1.refs_3_), custom_call_target="tpu_custom_call", output_to_operand_aliasing={{}: (3, {})} | custom-call | flops 201326592 | bytes 3145728 | tf_op jit(solution)/shard_map/merge1/pallas_call | solution.py:337
  (2 shorter events, 0.0 us)
Async XLA Ops:
  1.8 6.6 %collective-permute-start.23 = (bf16[16,2816]{1,0:T(8,128)(2,1)S(1)}, bf16[16,2816]{1,0:T(8,128)(2,1)S(1)}, u32[]{:S(2)}, u32[]{:S(2)}) collective-permute-start(bf16[16,2816]{1,0:T(8,128)(2,1)S(1)} %get-tuple-element.79), channel_id=1, source_target_pairs={{0,24},{8,16},{16,8},{24,0},{1,25},{9,17},{17,9},{25,1},{2,26},{10... | collective-permute-start | bytes 270344 | tf_op jit(solution)/shard_map/ppermute | solution.py:42
  4.9 4.6 %collective-permute-start.24 = (bf16[16,2816]{1,0:T(8,128)(2,1)S(1)}, bf16[16,2816]{1,0:T(8,128)(2,1)S(1)}, u32[]{:S(2)}, u32[]{:S(2)}) collective-permute-start(bf16[16,2816]{1,0:T(8,128)(2,1)S(1)} %get-tuple-element.80), channel_id=1, source_target_pairs={{0,8},{8,0},{16,24},{24,16},{1,9},{9,1},{17,25},{25,17},{2,10},{10... | collective-permute-start | bytes 270344 | tf_op jit(solution)/shard_map/ppermute | solution.py:42
  5.1 4.4 %collective-permute-start.25 = (bf16[16,2816]{1,0:T(8,128)(2,1)S(1)}, bf16[16,2816]{1,0:T(8,128)(2,1)S(1)}, u32[]{:S(2)}, u32[]{:S(2)}) collective-permute-start(bf16[16,2816]{1,0:T(8,128)(2,1)S(1)} %get-tuple-element.81), channel_id=1, source_target_pairs={{0,16},{8,24},{16,0},{24,8},{1,17},{9,25},{17,1},{25,9},{2,18},{10... | collective-permute-start | bytes 270344 | tf_op jit(solution)/shard_map/ppermute | solution.py:42
  9.7 5.3 %collective-permute-start.10 = (bf16[16,2816]{1,0:T(8,128)(2,1)S(1)}, bf16[16,2816]{1,0:T(8,128)(2,1)S(1)}, u32[]{:S(2)}, u32[]{:S(2)}) collective-permute-start(bf16[16,2816]{1,0:T(8,128)(2,1)S(1)} %param.11), channel_id=1, source_target_pairs={{0,2},{2,6},{4,12},{6,0},{8,10},{10,14},{12,4},{14,8},{16,18},{18,... | collective-permute-start | bytes 270344 | tf_op jit(solution)/shard_map/cond/branch_11_fun/ppermute | solution.py:278
  15.1 5.8 %collective-permute-start.28 = (bf16[16,2816]{1,0:T(8,128)(2,1)S(1)}, bf16[16,2816]{1,0:T(8,128)(2,1)S(1)}, u32[]{:S(2)}, u32[]{:S(2)}) collective-permute-start(bf16[16,2816]{1,0:T(8,128)(2,1)S(1)} %broadcast_select_fusion.refs_0_), channel_id=1, source_target_pairs={{0,24},{8,16},{16,8},{24,0},{1,25},{9,17},{17,9},{25,1},{2,26},{10... | collective-permute-start | bytes 270344 | tf_op jit(solution)/shard_map/ppermute | solution.py:42
  17.2 3.7 %collective-permute-start.27 = (bf16[16,2816]{1,0:T(8,128)(2,1)S(1)}, bf16[16,2816]{1,0:T(8,128)(2,1)S(1)}, u32[]{:S(2)}, u32[]{:S(2)}) collective-permute-start(bf16[16,2816]{1,0:T(8,128)(2,1)S(1)} %broadcast_select_fusion.refs_0_), channel_id=1, source_target_pairs={{0,8},{8,0},{16,24},{24,16},{1,9},{9,1},{17,25},{25,17},{2,10},{10... | collective-permute-start | bytes 270344 | tf_op jit(solution)/shard_map/ppermute | solution.py:42
  17.6 3.4 %collective-permute-start.26 = (bf16[16,2816]{1,0:T(8,128)(2,1)S(1)}, bf16[16,2816]{1,0:T(8,128)(2,1)S(1)}, u32[]{:S(2)}, u32[]{:S(2)}) collective-permute-start(bf16[16,2816]{1,0:T(8,128)(2,1)S(1)} %broadcast_select_fusion.refs_0_), channel_id=1, source_target_pairs={{0,16},{8,24},{16,0},{24,8},{1,17},{9,25},{17,1},{25,9},{2,18},{10... | collective-permute-start | bytes 270344 | tf_op jit(solution)/shard_map/ppermute | solution.py:42
  21.1 5.9 %collective-permute-start.29 = (bf16[64,2048]{1,0:T(8,128)(2,1)S(1)}, bf16[64,2048]{1,0:T(8,128)(2,1)S(1)}, u32[]{:S(2)}, u32[]{:S(2)}) collective-permute-start(bf16[64,2048]{1,0:T(8,128)(2,1)S(1)} %get-tuple-element.84.refs_1_), channel_id=1, source_target_pairs={{0,1},{1,0},{2,3},{3,2},{4,5},{5,4},{6,7},{7,6},{8,9},{9,8},{10,11... | collective-permute-start | bytes 786440 | tf_op jit(solution)/shard_map/ppermute | solution.py:42

commit v3 on v1

--- a/solution.py
+++ b/solution.py
@@ -54,8 +54,13 @@
     return pl.CostEstimate(flops=flops, bytes_accessed=nbytes, transcendentals=0)
 
 
+def halves_of(cols):
+    middle = -(-cols // 256) * 128
+    return [(0, middle), (middle, cols)]
+
+
 def pack_kernel(n_dp, ranks, cols_a, grad_a, grad_b, *refs):
-    outs, rows, sems = refs[: n_dp - 1], refs[n_dp - 1], refs[n_dp]
+    outs, rows, sems = refs[:-2], refs[-2], refs[-1]
     me = lax.axis_index("dp")
     copies = []
     for k in range(1, n_dp):
@@ -78,12 +83,13 @@
     for k, pair in enumerate(copies):
         for copy in pair:
             copy.wait()
-        outs[k][...] = rows[k].astype(BF16)
+        for half, (low, high) in enumerate(halves_of(rows.shape[2])):
+            outs[2 * k + half][...] = rows[k, :, low:high].astype(BF16)
 
 
 def load_kernel(ranks, cols_a, slots_in, *refs):
     grad_a, grad_b, fa, fb, ma, mb, sa, sb = refs[:8]
-    grad, factor, moment, second, order, slot_of, sems = refs[8:]
+    grad, factor, moment, second, order, stays, slot_of, sems = refs[8:]
     me = lax.axis_index("dp")
     start = pl.multiple_of(me * ranks, ranks)
     first = pl.ds(0, cols_a)
@@ -112,50 +118,58 @@
         number = number * (n - i) + smaller
     order[0] = number
     here = lax.axis_index("expert")
-    order[1] = (slot_of[here] == here).astype(jnp.int32)
+    stays[0] = (slot_of[here] == here).astype(jnp.int32)
     for copy in copies:
         copy.wait()
 
 
-def keep_kernel(piece, kept):
-    kept[...] = piece[...]
+def keep_kernel(*refs):
+    for piece, kept in zip(refs[:2], refs[2:]):
+        kept[...] = piece[...]
 
 
 def send_kernel(*refs):
     grad, factor, moment, second = refs[:4]
-    total = grad[...]
-    for piece in refs[4:-1]:
-        total = total + piece[...].astype(F32)
-    refs[-1][...] = adam_update(factor[...], moment[...], second[...], total)[0].astype(BF16)
+    for half, (low, high) in enumerate(halves_of(grad.shape[1])):
+        total = grad[:, low:high]
+        for piece in refs[4 + half : -2 : 2]:
+            total = total + piece[...].astype(F32)
+        new = adam_update(factor[:, low:high], moment[:, low:high], second[:, low:high], total)
+        refs[-2 + half][...] = new[0].astype(BF16)
 
 
 def state_kernel(n_got, cols_a, weight, *refs):
-    ins = refs[: 4 + n_got]
+    grad, factor, moment, second = refs[:4]
+    got = refs[4 : 4 + n_got]
     outs = refs[4 + n_got : 10 + n_got]
     panel = refs[10 + n_got]
     parts = refs[11 + n_got : 17 + n_got]
     sems = refs[-1]
-    cols_b = ins[0].shape[1] - cols_a
-    width = 256 if cols_a % 256 == 0 and cols_b % 256 == 0 else 128
+    width = 128
     load = pltpu.make_async_copy(weight.at[0], panel, sems.at[0])
     load.start()
 
-    def some_columns(start, into, at):
-        here = pl.ds(pl.multiple_of(start, width), width)
-        there = pl.ds(pl.multiple_of(at, width), width)
-        grad, factor, moment, second = (ref[:, here] for ref in ins[:4])
-        for piece in ins[4:]:
-            grad = grad + piece[:, here].astype(F32)
-        for out, new in zip(into, adam_update(factor, moment, second, grad)):
+    def some_columns(half, at, low, into, start):
+        here = pl.ds(pl.multiple_of(at, width), width)
+        inside = pl.ds(pl.multiple_of(at - low, width), width)
+        there = pl.ds(pl.multiple_of(start, width), width)
+        total = grad[:, here]
+        for piece in got[half::2]:
+            total = total + piece[:, inside].astype(F32)
+        for out, new in zip(
+            into, adam_update(factor[:, here], moment[:, here], second[:, here], total)
+        ):
             out[:, there] = new
 
-    @pl.loop(0, cols_a // width)
-    def _(i):
-        some_columns(i * width, parts[::2], i * width)
-
-    @pl.loop(0, cols_b // width)
-    def _(i):
-        some_columns(cols_a + i * width, parts[1::2], i * width)
+    for half, (low, high) in enumerate(halves_of(grad.shape[1])):
+
+        @pl.loop(low // width, min(high, cols_a) // width)
+        def _(i, half=half, low=low):
+            some_columns(half, i * width, low, parts[::2], i * width)
+
+        @pl.loop(max(low, cols_a) // width, high // width)
+        def _(i, half=half, low=low):
+            some_columns(half, i * width, low, parts[1::2], i * width - cols_a)
 
     copies = [
         pltpu.make_async_copy(part, out.at[0], sems.at[1 + i])
@@ -168,13 +182,18 @@
     load.wait()
 
 
-def join_kernel(cols_a, *refs):
+def join_kernel(cols_a, cols_b, *refs):
     parts = refs[:-4]
     rows_a, flipped = refs[-3:-1]
-    ranks = parts[0].shape[0]
-    for i, part in enumerate(parts):
-        rows_a[pl.ds(i * ranks, ranks), :] = part[:, :cols_a]
-    rows_b = jnp.concatenate([part[:, cols_a:].astype(F32) for part in parts], axis=0)
+    rows_b = []
+    for half, (low, high) in enumerate(halves_of(cols_a + cols_b)):
+        rows = jnp.concatenate([part[...].astype(F32) for part in parts[half::2]], axis=0)
+        edge = min(max(cols_a - low, 0), high - low)
+        if edge > 0:
+            rows_a[:, low : low + edge] = rows[:, :edge].astype(BF16)
+        if edge < high - low:
+            rows_b.append(rows[:, edge:])
+    rows_b = jnp.concatenate(rows_b, axis=1) if len(rows_b) > 1 else rows_b[0]
     flipped[...] = (rows_b * ADAPTER_SCALE).T.astype(BF16)
 
 
@@ -215,11 +234,12 @@
     cols_b = factor_b.shape[2]
     cols = cols_a + cols_b
 
+    shapes = [(ranks, high - low) for low, high in halves_of(cols)]
     pieces = pl.pallas_call(
         functools.partial(pack_kernel, n_dp, ranks, cols_a),
         in_specs=[HBM, HBM],
-        out_specs=[VMEM] * (n_dp - 1),
-        out_shape=[pltpu.VMEM((ranks, cols), BF16)] * (n_dp - 1),
+        out_specs=[VMEM] * (2 * n_dp - 2),
+        out_shape=[pltpu.VMEM(shape, BF16) for shape in shapes] * (n_dp - 1),
         scratch_shapes=[
             pltpu.VMEM((n_dp - 1, ranks, cols), F32),
             pltpu.SemaphoreType.DMA((n_dp - 1, 2)),
@@ -227,13 +247,17 @@
         compiler_params=PARAMS,
         name="pack",
     )(left(grad_a), left(grad_b))
-    got = [held(swap(pieces[k - 1], "dp", n_dp, k)) for k in range(n_dp - 1, 0, -1)]
-
-    *state, order = pl.pallas_call(
+    got = [
+        held(swap(pieces[2 * k - 2 + half], "dp", n_dp, k))
+        for k in range(n_dp - 1, 0, -1)
+        for half in range(2)
+    ]
+
+    *state, order, stays = pl.pallas_call(
         functools.partial(load_kernel, ranks, cols_a),
         in_specs=[HBM] * 9,
-        out_specs=[VMEM] * 4 + [SMEM],
-        out_shape=[pltpu.VMEM((ranks, cols), F32)] * 4 + [pltpu.SMEM((2,), jnp.int32)],
+        out_specs=[VMEM] * 4 + [SMEM] * 2,
+        out_shape=[pltpu.VMEM((ranks, cols), F32)] * 4 + [pltpu.SMEM((1,), jnp.int32)] * 2,
         scratch_shapes=[pltpu.SMEM(slot_of.shape, jnp.int32), pltpu.SemaphoreType.DMA((9,))],
         compiler_params=PARAMS,
         cost_estimate=estimate(4 * ranks * cols * 4),
@@ -258,9 +282,9 @@
 
     send = pl.pallas_call(
         send_kernel,
-        in_specs=[VMEM] * (3 + n_dp),
-        out_specs=VMEM,
-        out_shape=pltpu.VMEM((ranks, cols), BF16),
+        in_specs=[VMEM] * (2 + 2 * n_dp),
+        out_specs=[VMEM] * 2,
+        out_shape=[pltpu.VMEM(shape, BF16) for shape in shapes],
         compiler_params=PARAMS,
         name="send",
     )(*state, *got)
@@ -274,40 +298,47 @@
         moves = any(expert != slot for expert, slot in enumerate(slots))
 
         def branch(send):
-            mine = lax.ppermute(send, ("dp", "expert"), pairs) if moves else send
+            mine = send
+            if moves:
+                mine = [lax.ppermute(x, ("dp", "expert"), pairs) for x in send]
             return pl.pallas_call(
                 keep_kernel,
-                in_specs=[VMEM],
-                out_specs=VMEM,
-                out_shape=pltpu.VMEM((ranks, cols), BF16),
+                in_specs=[VMEM] * 2,
+                out_specs=[VMEM] * 2,
+                out_shape=[pltpu.VMEM(shape, BF16) for shape in shapes],
                 compiler_params=PARAMS,
                 name="keep",
-            )(held(mine))
+            )(*map(held, mine))
 
         return branch
 
     if n_expert <= MOST_SWITCHED:
         orders = itertools.permutations(range(n_expert))
         mine = lax.switch(order[0], [move(slots) for slots in orders], send)
-        mine = jnp.where(order[1] == 1, send, mine)
+        mine = [jnp.where(stays[0] == 1, a, b) for a, b in zip(send, mine)]
     else:
         mine = send
         here = lax.axis_index("expert")
         experts = jnp.arange(n_expert, dtype=jnp.int32)
         wanted = jnp.sum(jnp.where(slot_of == here, experts, 0)) ^ here
         for k in range(1, n_expert):
-            mine = jnp.where(wanted == k, swap(send, "expert", n_expert, k), mine)
-
-    parts = [mine] + [swap(mine, "dp", n_dp, k) for k in range(1, n_dp)]
+            mine = [
+                jnp.where(wanted == k, swap(a, "expert", n_expert, k), b)
+                for a, b in zip(send, mine)
+            ]
+
+    parts = list(mine)
+    for k in range(1, n_dp):
+        parts += [swap(x, "dp", n_dp, k) for x in mine]
     panel_shape = weight.shape[1:]
-    shapes = [factor_a.shape, factor_b.shape] * 3
+    full = [factor_a.shape, factor_b.shape] * 3
     *new, panel = pl.pallas_call(
-        functools.partial(state_kernel, n_dp - 1, cols_a),
-        in_specs=[HBM] + [VMEM] * (3 + n_dp),
+        functools.partial(state_kernel, 2 * n_dp - 2, cols_a),
+        in_specs=[HBM] + [VMEM] * (2 + 2 * n_dp),
         out_specs=[HBM] * 6 + [VMEM],
-        out_shape=[jax.ShapeDtypeStruct(shape, F32) for shape in shapes]
+        out_shape=[jax.ShapeDtypeStruct(shape, F32) for shape in full]
         + [pltpu.VMEM(panel_shape, BF16)],
-        scratch_shapes=[pltpu.VMEM(shape[1:], F32) for shape in shapes]
+        scratch_shapes=[pltpu.VMEM(shape[1:], F32) for shape in full]
         + [pltpu.SemaphoreType.DMA((7,))],
         compiler_params=PARAMS,
         cost_estimate=estimate(weight.size * 4),
@@ -315,15 +346,15 @@
     )(left(weight), *state, *got)
     new_a, new_b, new_moment_a, new_moment_b, new_second_a, new_second_b = new
     rows_a, flipped, panel = pl.pallas_call(
-        functools.partial(join_kernel, cols_a),
-        in_specs=[VMEM] * (n_dp + 1),
+        functools.partial(join_kernel, cols_a, cols_b),
+        in_specs=[VMEM] * (2 * n_dp + 1),
         out_specs=[VMEM] * 3,
         out_shape=[
             pltpu.VMEM((ranks * n_dp, cols_a), BF16),
             pltpu.VMEM((cols_b, ranks * n_dp), BF16),
             pltpu.VMEM(panel_shape, BF16),
         ],
-        input_output_aliases={n_dp: 2},
+        input_output_aliases={2 * n_dp: 2},
         compiler_params=PARAMS,
         name="join",
     )(*map(held, parts), held(panel))

time: 29.1 us -> 36 us (1.24)
  starting transfers between devices: 13.4 us -> 21.6 us
  between operations: 2.02 us -> 0.77 us
  waiting for transfers between devices: 3.25 us -> 3.88 us
  local copies, waits for them, and re-layouts: 0.6 us -> 0 us
    ppermute x7 -> x13, starting transfers between devices: 9.73 us -> 17.9 us  [swap(): return lax.ppermute(x, axis, [(i, i ^ k) for i in range(n)])]
    slice x1 -> x0, local copies, waits for them, and re-layouts: 0.6 us -> none  [per_device(): mine = jnp.where(order[1] == 1, send, mine)]
    ppermute x1 -> x2, waiting for transfers between devices: 2.02 us -> 2.39 us  [branch(): mine = [lax.ppermute(x, ('dp', 'expert'), pairs) for x in send]]
    ppermute x7 -> x13, waiting for transfers between devices: 1.22 us -> 1.49 us  [swap(): return lax.ppermute(x, axis, [(i, i ^ k) for i in range(n)])]
    ppermute x1 -> x2, starting transfers between devices: 3.66 us -> 3.65 us  [branch(): mine = [lax.ppermute(x, ('dp', 'expert'), pairs) for x in send]]
  transfers between devices with their start and end apart: 8 -> 15, of which waited for: 4 -> 4; matrix products, arithmetic and copies ran while one was open for 2% -> 0% of each run, Pallas kernels for 22% -> 17%
where the time goes in v3:
time: 36 us; the launch traced here: 36.2 us
  starting transfers between devices  21.6 us (60%)
  Pallas kernels  9.86 us (27%)
  waiting for transfers between devices  3.88 us (11%)
  between operations  0.77 us (2%)
    ppermute x13, starting transfers between devices, swap(): return lax.ppermute(x, axis, [(i, i ^ k) for i in range(n)])  17.9 us
    pallas_call x2, Pallas kernels, per_device(): pl.pallas_call(functools.partial(merge_kernel, k, width), in_specs=[VMEM]...  4.06 us
    ppermute x2, starting transfers between devices, branch(): mine = [lax.ppermute(x, ('dp', 'expert'), pairs) for x in send]  3.65 us
    pallas_call x1, Pallas kernels, per_device(): pl.pallas_call(functools.partial(state_kernel, 2 * n_dp - 2, cols_a), in_...  3.04 us
    ppermute x2, waiting for transfers between devices, branch(): mine = [lax.ppermute(x, ('dp', 'expert'), pairs) for x in send]  2.39 us
    ppermute x13, waiting for transfers between devices, swap(): return lax.ppermute(x, axis, [(i, i ^ k) for i in range(n)])  1.49 us
    pallas_call x1, Pallas kernels, per_device(): pl.pallas_call(functools.partial(load_kernel, ranks, cols_a), in_specs=[H...  1.25 us
    pallas_call x1, Pallas kernels, per_device(): pl.pallas_call(functools.partial(pack_kernel, n_dp, ranks, cols_a), in_sp...  1.16 us
  transfers between devices with their start and end apart: 15, of which 4 were waited for; matrix products, arithmetic and copies ran while one was open for 0% of the time, Pallas kernels for 17%

profile of v3, /device:TPU:1, one launch (start us, length us, event | category | flops | bytes accessed | tf_op | source)
XLA Modules:
  0.0 36.2 jit_solution(3599639568709610918)
XLA Ops:
  0.6 1.2 %pack.1 = (bf16[16,1408]{1,0:T(8,128)(2,1)S(1)}, bf16[16,1408]{1,0:T(8,128)(2,1)S(1)}, bf16[16,1408]{1,0:T(8,128)(2,1)S(1)}, bf16[16,1408]{1,0:T(8,128)(2,1)S(1)...) custom-call(f32[1,1,64,2048]{3,2,1,0:T(8,128)} %grad_a.1, f32[1,1,64,768]{3,2,1,0:T(8,128)} %grad_b.1), custom_call_target="tpu_custom_call" | custom-call | tf_op jit(solution)/shard_map/pack/pallas_call | solution.py:238
  1.8 3.1 %collective-permute-start.46 = (bf16[16,1408]{1,0:T(8,128)(2,1)S(1)}, bf16[16,1408]{1,0:T(8,128)(2,1)S(1)}, u32[]{:S(2)}, u32[]{:S(2)}) collective-permute-start(bf16[16,1408]{1,0:T(8,128)(2,1)S(1)} %get-tuple-element.182), channel_id=1, source_target_pairs={{0,24},{8,16},{16,8},{24,0},{1,25},{9,17},{17,9},{25,1},{2,26},{10... | collective-permute-start | bytes 135176 | tf_op jit(solution)/shard_map/ppermute | solution.py:42
  4.9 0.1 collective-permute-start.47
  4.9 1.4 %collective-permute-start.48 = (bf16[16,1408]{1,0:T(8,128)(2,1)S(1)}, bf16[16,1408]{1,0:T(8,128)(2,1)S(1)}, u32[]{:S(2)}, u32[]{:S(2)}) collective-permute-start(bf16[16,1408]{1,0:T(8,128)(2,1)S(1)} %get-tuple-element.184), channel_id=1, source_target_pairs={{0,16},{8,24},{16,0},{24,8},{1,17},{9,25},{17,1},{25,9},{2,18},{10... | collective-permute-start | bytes 135176 | tf_op jit(solution)/shard_map/ppermute | solution.py:42
  6.3 0.1 collective-permute-start.49
  6.4 1.3 %collective-permute-start.50 = (bf16[16,1408]{1,0:T(8,128)(2,1)S(1)}, bf16[16,1408]{1,0:T(8,128)(2,1)S(1)}, u32[]{:S(2)}, u32[]{:S(2)}) collective-permute-start(bf16[16,1408]{1,0:T(8,128)(2,1)S(1)} %get-tuple-element.186), channel_id=1, source_target_pairs={{0,8},{8,0},{16,24},{24,16},{1,9},{9,1},{17,25},{25,17},{2,10},{10... | collective-permute-start | bytes 135176 | tf_op jit(solution)/shard_map/ppermute | solution.py:42
  7.7 0.1 collective-permute-start.51
  7.9 1.3 %load.1 = (f32[16,2816]{1,0:T(8,128)S(1)}, f32[16,2816]{1,0:T(8,128)S(1)}, f32[16,2816]{1,0:T(8,128)S(1)}, f32[16,2816]{1,0:T(8,128)S(1)}, s32[1]{0:T(128)S(4)}, /*index=5*/s32[1]{0:T(128)S(4)}) custom-call(s32[4]{0:T(128)} %slots_in.1, f32[1,1,64,2048]{3,2,1,0:T(8,128)} %grad_a.1, f32[1,1,64,768]{3,2,1,0:T(8,128)} %grad_b.1, f32[1,16,2048]{2,1,0:T(8,128)} %refs_2_.1, ...), custom_call_target="tpu_custom_call" | custom-call | bytes 720896 | tf_op jit(solution)/shard_map/load/pallas_call | solution.py:256
  9.1 0.0 collective-permute-done.47.refs_5_
  9.2 0.8 %collective-permute-done.49.refs_7_ = bf16[16,1408]{1,0:T(8,128)(2,1)S(1)} collective-permute-done((bf16[16,1408]{1,0:T(8,128)(2,1)S(1)}, bf16[16,1408]{1,0:T(8,128)(2,1)S(1)}, u32[]{:S(2)}, u32[]{:S(2)}) %collective-permute-start.49) | collective-permute-done | bytes 45088 | tf_op jit(solution)/shard_map/ppermute | solution.py:42
  9.9 0.7 %collective-permute-done.51.refs_9_ = bf16[16,1408]{1,0:T(8,128)(2,1)S(1)} collective-permute-done((bf16[16,1408]{1,0:T(8,128)(2,1)S(1)}, bf16[16,1408]{1,0:T(8,128)(2,1)S(1)}, u32[]{:S(2)}, u32[]{:S(2)}) %collective-permute-start.51) | collective-permute-done | bytes 45088 | tf_op jit(solution)/shard_map/ppermute | solution.py:42
  10.6 0.2 send.1
  10.8 6.1 %conditional.1 = ((bf16[16,1408]{1,0:T(8,128)(2,1)S(1)}, bf16[16,1408]{1,0:T(8,128)(2,1)S(1)})) conditional(s32[]{:T(128)} %bitcast.1, (bf16[16,1408]{1,0:T(8,128)(2,1)S(1)}, bf16[16,1408]{1,0:T(8,128)(2,1)S(1)}) %send.1, (bf16[16,1408]{1,0:T(8,128)(2,1)S(1)}, bf16[16,1408]{1,0:T(8,128)(2,1)S(1)}) %send.1, ...), branch_computations={%region_0.0_spmd, %region_1.0_spmd, %region_2.0_spmd, %region_3.0_... | conditional | bytes 360536 | solution.py:317
  10.9 1.3 %collective-permute-start.20 = (bf16[16,1408]{1,0:T(8,128)(2,1)S(1)}, bf16[16,1408]{1,0:T(8,128)(2,1)S(1)}, u32[]{:S(2)}, u32[]{:S(2)}) collective-permute-start(bf16[16,1408]{1,0:T(8,128)(2,1)S(1)} %get-tuple-element.118), channel_id=1, source_target_pairs={{0,2},{2,6},{4,12},{6,0},{8,10},{10,14},{12,4},{14,8},{16,18},{18,... | collective-permute-start | bytes 135176 | tf_op jit(solution)/shard_map/cond/branch_11_fun/ppermute | solution.py:303
  12.2 2.3 %collective-permute-start.21 = (bf16[16,1408]{1,0:T(8,128)(2,1)S(1)}, bf16[16,1408]{1,0:T(8,128)(2,1)S(1)}, u32[]{:S(2)}, u32[]{:S(2)}) collective-permute-start(bf16[16,1408]{1,0:T(8,128)(2,1)S(1)} %get-tuple-element.119), channel_id=1, source_target_pairs={{0,2},{2,6},{4,12},{6,0},{8,10},{10,14},{12,4},{14,8},{16,18},{18,... | collective-permute-start | bytes 135176 | tf_op jit(solution)/shard_map/cond/branch_11_fun/ppermute | solution.py:303
  14.5 1.2 %collective-permute-done.20.refs_0_ = bf16[16,1408]{1,0:T(8,128)(2,1)S(1)} collective-permute-done((bf16[16,1408]{1,0:T(8,128)(2,1)S(1)}, bf16[16,1408]{1,0:T(8,128)(2,1)S(1)}, u32[]{:S(2)}, u32[]{:S(2)}) %collective-permute-start.20) | collective-permute-done | bytes 45088 | tf_op jit(solution)/shard_map/cond/branch_11_fun/ppermute | solution.py:303
  15.7 1.2 %collective-permute-done.21.refs_1_ = bf16[16,1408]{1,0:T(8,128)(2,1)S(1)} collective-permute-done((bf16[16,1408]{1,0:T(8,128)(2,1)S(1)}, bf16[16,1408]{1,0:T(8,128)(2,1)S(1)}, u32[]{:S(2)}, u32[]{:S(2)}) %collective-permute-start.21) | collective-permute-done | bytes 45088 | tf_op jit(solution)/shard_map/cond/branch_11_fun/ppermute | solution.py:303
  17.0 1.8 %collective-permute-start.57 = (bf16[16,1408]{1,0:T(8,128)(2,1)S(1)}, bf16[16,1408]{1,0:T(8,128)(2,1)S(1)}, u32[]{:S(2)}, u32[]{:S(2)}) collective-permute-start(bf16[16,1408]{1,0:T(8,128)(2,1)S(1)} %broadcast_select_fusion.refs_1_), channel_id=1, source_target_pairs={{0,24},{8,16},{16,8},{24,0},{1,25},{9,17},{17,9},{25,1},{2,26},{10... | collective-permute-start | bytes 135176 | tf_op jit(solution)/shard_map/ppermute | solution.py:42
  18.8 0.4 collective-permute-start.55
  19.1 0.6 %collective-permute-start.53 = (bf16[16,1408]{1,0:T(8,128)(2,1)S(1)}, bf16[16,1408]{1,0:T(8,128)(2,1)S(1)}, u32[]{:S(2)}, u32[]{:S(2)}) collective-permute-start(bf16[16,1408]{1,0:T(8,128)(2,1)S(1)} %broadcast_select_fusion.refs_1_), channel_id=1, source_target_pairs={{0,8},{8,0},{16,24},{24,16},{1,9},{9,1},{17,25},{25,17},{2,10},{10... | collective-permute-start | bytes 135176 | tf_op jit(solution)/shard_map/ppermute | solution.py:42
  19.7 1.8 %collective-permute-start.56 = (bf16[16,1408]{1,0:T(8,128)(2,1)S(1)}, bf16[16,1408]{1,0:T(8,128)(2,1)S(1)}, u32[]{:S(2)}, u32[]{:S(2)}) collective-permute-start(bf16[16,1408]{1,0:T(8,128)(2,1)S(1)} %broadcast_select_fusion.1.refs_0_), channel_id=1, source_target_pairs={{0,24},{8,16},{16,8},{24,0},{1,25},{9,17},{17,9},{25,1},{2,26},{10... | collective-permute-start | bytes 135176 | tf_op jit(solution)/shard_map/ppermute | solution.py:42
  21.5 0.4 collective-permute-start.54
  21.8 0.6 %collective-permute-start.52 = (bf16[16,1408]{1,0:T(8,128)(2,1)S(1)}, bf16[16,1408]{1,0:T(8,128)(2,1)S(1)}, u32[]{:S(2)}, u32[]{:S(2)}) collective-permute-start(bf16[16,1408]{1,0:T(8,128)(2,1)S(1)} %broadcast_select_fusion.1.refs_0_), channel_id=1, source_target_pairs={{0,8},{8,0},{16,24},{24,16},{1,9},{9,1},{17,25},{25,17},{2,10},{10... | collective-permute-start | bytes 135176 | tf_op jit(solution)/shard_map/ppermute | solution.py:42
  22.4 3.0 %state.1 = (f32[1,16,2048]{2,1,0:T(8,128)}, f32[1,16,768]{2,1,0:T(8,128)}, f32[1,16,2048]{2,1,0:T(8,128)}, f32[1,16,768]{2,1,0:T(8,128)}, f32[1,16,2048]{2,1,0:T...) custom-call(bf16[1,768,4096]{2,1,0:T(8,128)(2,1)} %weight.1, f32[16,2816]{1,0:T(8,128)S(1)} %get-tuple-element.178.refs_0_, ...), custom_call_target="tpu_custom_call" | custom-call | bytes 12582912 | tf_op jit(solution)/shard_map/state/pallas_call | solution.py:335
  25.5 0.0 collective-permute-done.53.refs_3_
  25.5 0.0 collective-permute-done.56.refs_6_
  25.5 0.0 collective-permute-done.52.refs_2_
  25.5 0.2 join.1
  25.7 6.4 %collective-permute-start.58 = (bf16[64,2048]{1,0:T(8,128)(2,1)S(1)}, bf16[64,2048]{1,0:T(8,128)(2,1)S(1)}, u32[]{:S(2)}, u32[]{:S(2)}) collective-permute-start(bf16[64,2048]{1,0:T(8,128)(2,1)S(1)} %get-tuple-element.195.refs_1_), channel_id=1, source_target_pairs={{0,1},{1,0},{2,3},{3,2},{4,5},{5,4},{6,7},{7,6},{8,9},{9,8},{10,11... | collective-permute-start | bytes 786440 | tf_op jit(solution)/shard_map/ppermute | solution.py:42
  32.1 2.0 %merge0.1.refs_3_ = bf16[1,768,4096]{2,1,0:T(8,128)(2,1)} custom-call(bf16[768,4096]{1,0:T(8,128)(2,1)S(1)} %get-tuple-element.194.refs_0_, bf16[64,2048]{1,0:T(8,128)(2,1)S(1)} %get-tuple-element.195.refs_1_, bf16[768,64]{1,0:T(8,128)(2,1)S(1)} %get-tuple-element.196.refs_2_), custom_call_target="tpu_custom_call" | custom-call | flops 201326592 | bytes 3145728 | tf_op jit(solution)/shard_map/merge0/pallas_call | solution.py:367
  34.1 0.0 collective-permute-done.58.refs_1_
  34.1 2.0 %merge1.1 = bf16[1,768,4096]{2,1,0:T(8,128)(2,1)} custom-call(bf16[768,4096]{1,0:T(8,128)(2,1)S(1)} %get-tuple-element.194.refs_0_, bf16[64,2048]{1,0:T(8,128)(2,1)S(1)} %collective-permute-done.58.refs_1_, bf16[768,64]{1,0:T(8,128)(2,1)S(1)} %get-tuple-element.196.refs_2_, bf16[1,768,4096]{2,1,0:T(8,128)(2,1)} %merge0.1.refs_3_), custom_call_target="tpu_custom_call", output_to_operand_aliasing={{}: (3, {})} | custom-call | flops 201326592 | bytes 3145728 | tf_op jit(solution)/shard_map/merge1/pallas_call | solution.py:367
  (9 shorter events, 0.0 us)
Async XLA Ops:
  1.8 5.9 %collective-permute-start.46 = (bf16[16,1408]{1,0:T(8,128)(2,1)S(1)}, bf16[16,1408]{1,0:T(8,128)(2,1)S(1)}, u32[]{:S(2)}, u32[]{:S(2)}) collective-permute-start(bf16[16,1408]{1,0:T(8,128)(2,1)S(1)} %get-tuple-element.182), channel_id=1, source_target_pairs={{0,24},{8,16},{16,8},{24,0},{1,25},{9,17},{17,9},{25,1},{2,26},{10... | collective-permute-start | bytes 135176 | tf_op jit(solution)/shard_map/ppermute | solution.py:42
  4.9 4.3 %collective-permute-start.47 = (bf16[16,1408]{1,0:T(8,128)(2,1)S(1)}, bf16[16,1408]{1,0:T(8,128)(2,1)S(1)}, u32[]{:S(2)}, u32[]{:S(2)}) collective-permute-start(bf16[16,1408]{1,0:T(8,128)(2,1)S(1)} %get-tuple-element.183), channel_id=1, source_target_pairs={{0,24},{8,16},{16,8},{24,0},{1,25},{9,17},{17,9},{25,1},{2,26},{10... | collective-permute-start | bytes 135176 | tf_op jit(solution)/shard_map/ppermute | solution.py:42
  4.9 4.2 %collective-permute-start.48 = (bf16[16,1408]{1,0:T(8,128)(2,1)S(1)}, bf16[16,1408]{1,0:T(8,128)(2,1)S(1)}, u32[]{:S(2)}, u32[]{:S(2)}) collective-permute-start(bf16[16,1408]{1,0:T(8,128)(2,1)S(1)} %get-tuple-element.184), channel_id=1, source_target_pairs={{0,16},{8,24},{16,0},{24,8},{1,17},{9,25},{17,1},{25,9},{2,18},{10... | collective-permute-start | bytes 135176 | tf_op jit(solution)/shard_map/ppermute | solution.py:42
  6.3 3.6 %collective-permute-start.49 = (bf16[16,1408]{1,0:T(8,128)(2,1)S(1)}, bf16[16,1408]{1,0:T(8,128)(2,1)S(1)}, u32[]{:S(2)}, u32[]{:S(2)}) collective-permute-start(bf16[16,1408]{1,0:T(8,128)(2,1)S(1)} %get-tuple-element.185), channel_id=1, source_target_pairs={{0,16},{8,24},{16,0},{24,8},{1,17},{9,25},{17,1},{25,9},{2,18},{10... | collective-permute-start | bytes 135176 | tf_op jit(solution)/shard_map/ppermute | solution.py:42
  6.4 3.5 %collective-permute-start.50 = (bf16[16,1408]{1,0:T(8,128)(2,1)S(1)}, bf16[16,1408]{1,0:T(8,128)(2,1)S(1)}, u32[]{:S(2)}, u32[]{:S(2)}) collective-permute-start(bf16[16,1408]{1,0:T(8,128)(2,1)S(1)} %get-tuple-element.186), channel_id=1, source_target_pairs={{0,8},{8,0},{16,24},{24,16},{1,9},{9,1},{17,25},{25,17},{2,10},{10... | collective-permute-start | bytes 135176 | tf_op jit(solution)/shard_map/ppermute | solution.py:42
  7.7 2.9 %collective-permute-start.51 = (bf16[16,1408]{1,0:T(8,128)(2,1)S(1)}, bf16[16,1408]{1,0:T(8,128)(2,1)S(1)}, u32[]{:S(2)}, u32[]{:S(2)}) collective-permute-start(bf16[16,1408]{1,0:T(8,128)(2,1)S(1)} %get-tuple-element.187), channel_id=1, source_target_pairs={{0,8},{8,0},{16,24},{24,16},{1,9},{9,1},{17,25},{25,17},{2,10},{10... | collective-permute-start | bytes 135176 | tf_op jit(solution)/shard_map/ppermute | solution.py:42
  10.9 4.8 %collective-permute-start.20 = (bf16[16,1408]{1,0:T(8,128)(2,1)S(1)}, bf16[16,1408]{1,0:T(8,128)(2,1)S(1)}, u32[]{:S(2)}, u32[]{:S(2)}) collective-permute-start(bf16[16,1408]{1,0:T(8,128)(2,1)S(1)} %get-tuple-element.118), channel_id=1, source_target_pairs={{0,2},{2,6},{4,12},{6,0},{8,10},{10,14},{12,4},{14,8},{16,18},{18,... | collective-permute-start | bytes 135176 | tf_op jit(solution)/shard_map/cond/branch_11_fun/ppermute | solution.py:303
  12.2 4.7 %collective-permute-start.21 = (bf16[16,1408]{1,0:T(8,128)(2,1)S(1)}, bf16[16,1408]{1,0:T(8,128)(2,1)S(1)}, u32[]{:S(2)}, u32[]{:S(2)}) collective-permute-start(bf16[16,1408]{1,0:T(8,128)(2,1)S(1)} %get-tuple-element.119), channel_id=1, source_target_pairs={{0,2},{2,6},{4,12},{6,0},{8,10},{10,14},{12,4},{14,8},{16,18},{18,... | collective-permute-start | bytes 135176 | tf_op jit(solution)/shard_map/cond/branch_11_fun/ppermute | solution.py:303
  17.0 4.9 %collective-permute-start.57 = (bf16[16,1408]{1,0:T(8,128)(2,1)S(1)}, bf16[16,1408]{1,0:T(8,128)(2,1)S(1)}, u32[]{:S(2)}, u32[]{:S(2)}) collective-permute-start(bf16[16,1408]{1,0:T(8,128)(2,1)S(1)} %broadcast_select_fusion.refs_1_), channel_id=1, source_target_pairs={{0,24},{8,16},{16,8},{24,0},{1,25},{9,17},{17,9},{25,1},{2,26},{10... | collective-permute-start | bytes 135176 | tf_op jit(solution)/shard_map/ppermute | solution.py:42
  18.8 6.7 %collective-permute-start.55 = (bf16[16,1408]{1,0:T(8,128)(2,1)S(1)}, bf16[16,1408]{1,0:T(8,128)(2,1)S(1)}, u32[]{:S(2)}, u32[]{:S(2)}) collective-permute-start(bf16[16,1408]{1,0:T(8,128)(2,1)S(1)} %broadcast_select_fusion.refs_1_), channel_id=1, source_target_pairs={{0,16},{8,24},{16,0},{24,8},{1,17},{9,25},{17,1},{25,9},{2,18},{10... | collective-permute-start | bytes 135176 | tf_op jit(solution)/shard_map/ppermute | solution.py:42
  19.1 6.4 %collective-permute-start.53 = (bf16[16,1408]{1,0:T(8,128)(2,1)S(1)}, bf16[16,1408]{1,0:T(8,128)(2,1)S(1)}, u32[]{:S(2)}, u32[]{:S(2)}) collective-permute-start(bf16[16,1408]{1,0:T(8,128)(2,1)S(1)} %broadcast_select_fusion.refs_1_), channel_id=1, source_target_pairs={{0,8},{8,0},{16,24},{24,16},{1,9},{9,1},{17,25},{25,17},{2,10},{10... | collective-permute-start | bytes 135176 | tf_op jit(solution)/shard_map/ppermute | solution.py:42
  19.7 5.8 %collective-permute-start.56 = (bf16[16,1408]{1,0:T(8,128)(2,1)S(1)}, bf16[16,1408]{1,0:T(8,128)(2,1)S(1)}, u32[]{:S(2)}, u32[]{:S(2)}) collective-permute-start(bf16[16,1408]{1,0:T(8,128)(2,1)S(1)} %broadcast_select_fusion.1.refs_0_), channel_id=1, source_target_pairs={{0,24},{8,16},{16,8},{24,0},{1,25},{9,17},{17,9},{25,1},{2,26},{10... | collective-permute-start | bytes 135176 | tf_op jit(solution)/shard_map/ppermute | solution.py:42
  21.5 4.0 %collective-permute-start.54 = (bf16[16,1408]{1,0:T(8,128)(2,1)S(1)}, bf16[16,1408]{1,0:T(8,128)(2,1)S(1)}, u32[]{:S(2)}, u32[]{:S(2)}) collective-permute-start(bf16[16,1408]{1,0:T(8,128)(2,1)S(1)} %broadcast_select_fusion.1.refs_0_), channel_id=1, source_target_pairs={{0,16},{8,24},{16,0},{24,8},{1,17},{9,25},{17,1},{25,9},{2,18},{10... | collective-permute-start | bytes 135176 | tf_op jit(solution)/shard_map/ppermute | solution.py:42
  21.8 3.7 %collective-permute-start.52 = (bf16[16,1408]{1,0:T(8,128)(2,1)S(1)}, bf16[16,1408]{1,0:T(8,128)(2,1)S(1)}, u32[]{:S(2)}, u32[]{:S(2)}) collective-permute-start(bf16[16,1408]{1,0:T(8,128)(2,1)S(1)} %broadcast_select_fusion.1.refs_0_), channel_id=1, source_target_pairs={{0,8},{8,0},{16,24},{24,16},{1,9},{9,1},{17,25},{25,17},{2,10},{10... | collective-permute-start | bytes 135176 | tf_op jit(solution)/shard_map/ppermute | solution.py:42
  25.7 8.4 %collective-permute-start.58 = (bf16[64,2048]{1,0:T(8,128)(2,1)S(1)}, bf16[64,2048]{1,0:T(8,128)(2,1)S(1)}, u32[]{:S(2)}, u32[]{:S(2)}) collective-permute-start(bf16[64,2048]{1,0:T(8,128)(2,1)S(1)} %get-tuple-element.195.refs_1_), channel_id=1, source_target_pairs={{0,1},{1,0},{2,3},{3,2},{4,5},{5,4},{6,7},{7,6},{8,9},{9,8},{10,11... | collective-permute-start | bytes 786440 | tf_op jit(solution)/shard_map/ppermute | solution.py:42

commit v4 on v1

--- a/solution.py
+++ b/solution.py
@@ -83,7 +83,7 @@
 
 def load_kernel(ranks, cols_a, slots_in, *refs):
     grad_a, grad_b, fa, fb, ma, mb, sa, sb = refs[:8]
-    grad, factor, moment, second, order, slot_of, sems = refs[8:]
+    grad, factor, moment, second, order, stays, slot_of, sems = refs[8:]
     me = lax.axis_index("dp")
     start = pl.multiple_of(me * ranks, ranks)
     first = pl.ds(0, cols_a)
@@ -112,7 +112,7 @@
         number = number * (n - i) + smaller
     order[0] = number
     here = lax.axis_index("expert")
-    order[1] = (slot_of[here] == here).astype(jnp.int32)
+    stays[0] = (slot_of[here] == here).astype(jnp.int32)
     for copy in copies:
         copy.wait()
 
@@ -229,11 +229,11 @@
     )(left(grad_a), left(grad_b))
     got = [held(swap(pieces[k - 1], "dp", n_dp, k)) for k in range(n_dp - 1, 0, -1)]
 
-    *state, order = pl.pallas_call(
+    *state, order, stays = pl.pallas_call(
         functools.partial(load_kernel, ranks, cols_a),
         in_specs=[HBM] * 9,
-        out_specs=[VMEM] * 4 + [SMEM],
-        out_shape=[pltpu.VMEM((ranks, cols), F32)] * 4 + [pltpu.SMEM((2,), jnp.int32)],
+        out_specs=[VMEM] * 4 + [SMEM] * 2,
+        out_shape=[pltpu.VMEM((ranks, cols), F32)] * 4 + [pltpu.SMEM((1,), jnp.int32)] * 2,
         scratch_shapes=[pltpu.SMEM(slot_of.shape, jnp.int32), pltpu.SemaphoreType.DMA((9,))],
         compiler_params=PARAMS,
         cost_estimate=estimate(4 * ranks * cols * 4),
@@ -289,7 +289,7 @@
     if n_expert <= MOST_SWITCHED:
         orders = itertools.permutations(range(n_expert))
         mine = lax.switch(order[0], [move(slots) for slots in orders], send)
-        mine = jnp.where(order[1] == 1, send, mine)
+        mine = jnp.where(stays[0] == 1, send, mine)
     else:
         mine = send
         here = lax.axis_index("expert")

time: 29.1 us -> 28.4 us (0.976)
  waiting for transfers between devices: 3.25 us -> 6.09 us
  starting transfers between devices: 13.4 us -> 11.5 us
  between operations: 2.02 us -> 0.72 us
  local copies, waits for them, and re-layouts: 0.6 us -> 0 us
    ppermute x1, starting transfers between devices: 3.66 us -> 1.62 us  [branch(): mine = lax.ppermute(send, ('dp', 'expert'), pairs) if moves else send]
    ppermute x7, waiting for transfers between devices: 1.22 us -> 3.16 us  [swap(): return lax.ppermute(x, axis, [(i, i ^ k) for i in range(n)])]
    ppermute x1, waiting for transfers between devices: 2.02 us -> 2.93 us  [branch(): mine = lax.ppermute(send, ('dp', 'expert'), pairs) if moves else send]
    slice x1 -> x0, local copies, waits for them, and re-layouts: 0.6 us -> none  [per_device(): mine = jnp.where(order[1] == 1, send, mine)]
  transfers between devices with their start and end apart: 8 -> 8, of which waited for: 4 -> 5; matrix products, arithmetic and copies ran while one was open for 2% -> 0% of each run, Pallas kernels for 22% -> 22%
where the time goes in v4:
time: 28.4 us; the launch traced here: 28.2 us
  starting transfers between devices  11.5 us (40%)
  Pallas kernels  9.84 us (35%)
  waiting for transfers between devices  6.09 us (21%)
  between operations  0.72 us (3%)
    ppermute x7, starting transfers between devices, swap(): return lax.ppermute(x, axis, [(i, i ^ k) for i in range(n)])  9.86 us
    pallas_call x2, Pallas kernels, per_device(): pl.pallas_call(functools.partial(merge_kernel, k, width), in_specs=[VMEM]...  4.06 us
    ppermute x7, waiting for transfers between devices, swap(): return lax.ppermute(x, axis, [(i, i ^ k) for i in range(n)])  3.16 us
    pallas_call x1, Pallas kernels, per_device(): pl.pallas_call(functools.partial(state_kernel, n_dp - 1, cols_a), in_spec...  3.04 us
    ppermute x1, waiting for transfers between devices, branch(): mine = lax.ppermute(send, ('dp', 'expert'), pairs) if moves else send  2.93 us
    ppermute x1, starting transfers between devices, branch(): mine = lax.ppermute(send, ('dp', 'expert'), pairs) if moves else send  1.62 us
    pallas_call x1, Pallas kernels, per_device(): pl.pallas_call(functools.partial(load_kernel, ranks, cols_a), in_specs=[H...  1.25 us
    pallas_call x1, Pallas kernels, per_device(): pl.pallas_call(functools.partial(pack_kernel, n_dp, ranks, cols_a), in_sp...  1.16 us
  transfers between devices with their start and end apart: 8, of which 5 were waited for; matrix products, arithmetic and copies ran while one was open for 0% of the time, Pallas kernels for 22%

profile of v4, /device:TPU:1, one launch (start us, length us, event | category | flops | bytes accessed | tf_op | source)
XLA Modules:
  0.0 28.2 jit_solution(7064898892400885092)
XLA Ops:
  0.6 1.2 %pack.1 = (bf16[16,2816]{1,0:T(8,128)(2,1)S(1)}, bf16[16,2816]{1,0:T(8,128)(2,1)S(1)}, bf16[16,2816]{1,0:T(8,128)(2,1)S(1)}) custom-call(f32[1,1,64,2048]{3,2,1,0:T(8,128)} %grad_a.1, f32[1,1,64,768]{3,2,1,0:T(8,128)} %grad_b.1), custom_call_target="tpu_custom_call" | custom-call | tf_op jit(solution)/shard_map/pack/pallas_call | solution.py:218
  1.8 3.1 %collective-permute-start.23 = (bf16[16,2816]{1,0:T(8,128)(2,1)S(1)}, bf16[16,2816]{1,0:T(8,128)(2,1)S(1)}, u32[]{:S(2)}, u32[]{:S(2)}) collective-permute-start(bf16[16,2816]{1,0:T(8,128)(2,1)S(1)} %get-tuple-element.80), channel_id=1, source_target_pairs={{0,24},{8,16},{16,8},{24,0},{1,25},{9,17},{17,9},{25,1},{2,26},{10... | collective-permute-start | bytes 270344 | tf_op jit(solution)/shard_map/ppermute | solution.py:42
  4.9 0.2 collective-permute-start.24
  5.1 0.1 collective-permute-start.25
  5.2 1.3 %load.1 = (f32[16,2816]{1,0:T(8,128)S(1)}, f32[16,2816]{1,0:T(8,128)S(1)}, f32[16,2816]{1,0:T(8,128)S(1)}, f32[16,2816]{1,0:T(8,128)S(1)}, s32[1]{0:T(128)S(4)}, /*index=5*/s32[1]{0:T(128)S(4)}) custom-call(s32[4]{0:T(128)} %slots_in.1, f32[1,1,64,2048]{3,2,1,0:T(8,128)} %grad_a.1, f32[1,1,64,768]{3,2,1,0:T(8,128)} %grad_b.1, f32[1,16,2048]{2,1,0:T(8,128)} %refs_2_.1, ...), custom_call_target="tpu_custom_call" | custom-call | bytes 720896 | tf_op jit(solution)/shard_map/load/pallas_call | solution.py:232
  6.5 0.7 %collective-permute-done.23.refs_4_ = bf16[16,2816]{1,0:T(8,128)(2,1)S(1)} collective-permute-done((bf16[16,2816]{1,0:T(8,128)(2,1)S(1)}, bf16[16,2816]{1,0:T(8,128)(2,1)S(1)}, u32[]{:S(2)}, u32[]{:S(2)}) %collective-permute-start.23) | collective-permute-done | bytes 90144 | tf_op jit(solution)/shard_map/ppermute | solution.py:42
  7.2 1.7 %collective-permute-done.24.refs_5_ = bf16[16,2816]{1,0:T(8,128)(2,1)S(1)} collective-permute-done((bf16[16,2816]{1,0:T(8,128)(2,1)S(1)}, bf16[16,2816]{1,0:T(8,128)(2,1)S(1)}, u32[]{:S(2)}, u32[]{:S(2)}) %collective-permute-start.24) | collective-permute-done | bytes 90144 | tf_op jit(solution)/shard_map/ppermute | solution.py:42
  8.9 0.5 %collective-permute-done.25.refs_6_ = bf16[16,2816]{1,0:T(8,128)(2,1)S(1)} collective-permute-done((bf16[16,2816]{1,0:T(8,128)(2,1)S(1)}, bf16[16,2816]{1,0:T(8,128)(2,1)S(1)}, u32[]{:S(2)}, u32[]{:S(2)}) %collective-permute-start.25) | collective-permute-done | bytes 90144 | tf_op jit(solution)/shard_map/ppermute | solution.py:42
  9.4 0.2 send.1
  9.6 4.6 %conditional.1 = (bf16[16,2816]{1,0:T(8,128)(2,1)S(1)}) conditional(s32[]{:T(128)} %bitcast.1, bf16[16,2816]{1,0:T(8,128)(2,1)S(1)} %send.1, bf16[16,2816]{1,0:T(8,128)(2,1)S(1)} %send.1, bf16[16,2816]{1,0:T(8,128)(2,1)S(1)} %send.1, bf16[16,2816]{1,0:T(8,128)(2,1)S(1)} %send.1, ...), branch_computations={%region_0.0_spmd, %region_1.0_spmd, %region_2.0_spmd, %region_3.0_... | conditional | bytes 360496 | solution.py:291
  9.7 1.6 %collective-permute-start.7 = (bf16[16,2816]{1,0:T(8,128)(2,1)S(1)}, bf16[16,2816]{1,0:T(8,128)(2,1)S(1)}, u32[]{:S(2)}, u32[]{:S(2)}) collective-permute-start(bf16[16,2816]{1,0:T(8,128)(2,1)S(1)} %param.8), channel_id=1, source_target_pairs={{0,2},{2,4},{4,0},{6,14},{8,10},{10,12},{12,8},{14,6},{16,18},{18,... | collective-permute-start | bytes 270344 | tf_op jit(solution)/shard_map/cond/branch_8_fun/ppermute | solution.py:277
  11.3 2.9 %collective-permute-done.7.piece = bf16[16,2816]{1,0:T(8,128)(2,1)S(1)} collective-permute-done((bf16[16,2816]{1,0:T(8,128)(2,1)S(1)}, bf16[16,2816]{1,0:T(8,128)(2,1)S(1)}, u32[]{:S(2)}, u32[]{:S(2)}) %collective-permute-start.7) | collective-permute-done | bytes 90144 | tf_op jit(solution)/shard_map/cond/branch_8_fun/ppermute | solution.py:277
  14.2 1.0 %collective-permute-start.28 = (bf16[16,2816]{1,0:T(8,128)(2,1)S(1)}, bf16[16,2816]{1,0:T(8,128)(2,1)S(1)}, u32[]{:S(2)}, u32[]{:S(2)}) collective-permute-start(bf16[16,2816]{1,0:T(8,128)(2,1)S(1)} %broadcast_select_fusion.refs_0_), channel_id=1, source_target_pairs={{0,24},{8,16},{16,8},{24,0},{1,25},{9,17},{17,9},{25,1},{2,26},{10... | collective-permute-start | bytes 270344 | tf_op jit(solution)/shard_map/ppermute | solution.py:42
  15.2 1.6 %collective-permute-start.27 = (bf16[16,2816]{1,0:T(8,128)(2,1)S(1)}, bf16[16,2816]{1,0:T(8,128)(2,1)S(1)}, u32[]{:S(2)}, u32[]{:S(2)}) collective-permute-start(bf16[16,2816]{1,0:T(8,128)(2,1)S(1)} %broadcast_select_fusion.refs_0_), channel_id=1, source_target_pairs={{0,16},{8,24},{16,0},{24,8},{1,17},{9,25},{17,1},{25,9},{2,18},{10... | collective-permute-start | bytes 270344 | tf_op jit(solution)/shard_map/ppermute | solution.py:42
  16.9 0.1 collective-permute-start.26
  17.0 3.0 %state.1 = (f32[1,16,2048]{2,1,0:T(8,128)}, f32[1,16,768]{2,1,0:T(8,128)}, f32[1,16,2048]{2,1,0:T(8,128)}, f32[1,16,768]{2,1,0:T(8,128)}, f32[1,16,2048]{2,1,0:T...) custom-call(bf16[1,768,4096]{2,1,0:T(8,128)(2,1)} %weight.1, f32[16,2816]{1,0:T(8,128)S(1)} %get-tuple-element.76.refs_0_, ...), custom_call_target="tpu_custom_call" | custom-call | bytes 12582912 | tf_op jit(solution)/shard_map/state/pallas_call | solution.py:304
  20.0 0.0 collective-permute-done.28.refs_3_
  20.0 0.0 collective-permute-done.27.refs_2_
  20.0 0.2 collective-permute-done.26.refs_1_
  20.3 0.1 join.1
  20.4 3.7 %collective-permute-start.29 = (bf16[64,2048]{1,0:T(8,128)(2,1)S(1)}, bf16[64,2048]{1,0:T(8,128)(2,1)S(1)}, u32[]{:S(2)}, u32[]{:S(2)}) collective-permute-start(bf16[64,2048]{1,0:T(8,128)(2,1)S(1)} %get-tuple-element.86.refs_1_), channel_id=1, source_target_pairs={{0,1},{1,0},{2,3},{3,2},{4,5},{5,4},{6,7},{7,6},{8,9},{9,8},{10,11... | collective-permute-start | bytes 786440 | tf_op jit(solution)/shard_map/ppermute | solution.py:42
  24.1 2.0 %merge0.1.refs_3_ = bf16[1,768,4096]{2,1,0:T(8,128)(2,1)} custom-call(bf16[768,4096]{1,0:T(8,128)(2,1)S(1)} %get-tuple-element.85.refs_0_, bf16[64,2048]{1,0:T(8,128)(2,1)S(1)} %get-tuple-element.86.refs_1_, bf16[768,64]{1,0:T(8,128)(2,1)S(1)} %get-tuple-element.87.refs_2_), custom_call_target="tpu_custom_call" | custom-call | flops 201326592 | bytes 3145728 | tf_op jit(solution)/shard_map/merge0/pallas_call | solution.py:336
  26.2 0.0 collective-permute-done.29.refs_1_
  26.2 2.0 %merge1.1 = bf16[1,768,4096]{2,1,0:T(8,128)(2,1)} custom-call(bf16[768,4096]{1,0:T(8,128)(2,1)S(1)} %get-tuple-element.85.refs_0_, bf16[64,2048]{1,0:T(8,128)(2,1)S(1)} %collective-permute-done.29.refs_1_, bf16[768,64]{1,0:T(8,128)(2,1)S(1)} %get-tuple-element.87.refs_2_, bf16[1,768,4096]{2,1,0:T(8,128)(2,1)} %merge0.1.refs_3_), custom_call_target="tpu_custom_call", output_to_operand_aliasing={{}: (3, {})} | custom-call | flops 201326592 | bytes 3145728 | tf_op jit(solution)/shard_map/merge1/pallas_call | solution.py:336
  (2 shorter events, 0.0 us)
Async XLA Ops:
  1.8 5.4 %collective-permute-start.23 = (bf16[16,2816]{1,0:T(8,128)(2,1)S(1)}, bf16[16,2816]{1,0:T(8,128)(2,1)S(1)}, u32[]{:S(2)}, u32[]{:S(2)}) collective-permute-start(bf16[16,2816]{1,0:T(8,128)(2,1)S(1)} %get-tuple-element.80), channel_id=1, source_target_pairs={{0,24},{8,16},{16,8},{24,0},{1,25},{9,17},{17,9},{25,1},{2,26},{10... | collective-permute-start | bytes 270344 | tf_op jit(solution)/shard_map/ppermute | solution.py:42
  4.9 4.1 %collective-permute-start.24 = (bf16[16,2816]{1,0:T(8,128)(2,1)S(1)}, bf16[16,2816]{1,0:T(8,128)(2,1)S(1)}, u32[]{:S(2)}, u32[]{:S(2)}) collective-permute-start(bf16[16,2816]{1,0:T(8,128)(2,1)S(1)} %get-tuple-element.81), channel_id=1, source_target_pairs={{0,16},{8,24},{16,0},{24,8},{1,17},{9,25},{17,1},{25,9},{2,18},{10... | collective-permute-start | bytes 270344 | tf_op jit(solution)/shard_map/ppermute | solution.py:42
  5.1 4.3 %collective-permute-start.25 = (bf16[16,2816]{1,0:T(8,128)(2,1)S(1)}, bf16[16,2816]{1,0:T(8,128)(2,1)S(1)}, u32[]{:S(2)}, u32[]{:S(2)}) collective-permute-start(bf16[16,2816]{1,0:T(8,128)(2,1)S(1)} %get-tuple-element.82), channel_id=1, source_target_pairs={{0,8},{8,0},{16,24},{24,16},{1,9},{9,1},{17,25},{25,17},{2,10},{10... | collective-permute-start | bytes 270344 | tf_op jit(solution)/shard_map/ppermute | solution.py:42
  9.7 4.5 %collective-permute-start.7 = (bf16[16,2816]{1,0:T(8,128)(2,1)S(1)}, bf16[16,2816]{1,0:T(8,128)(2,1)S(1)}, u32[]{:S(2)}, u32[]{:S(2)}) collective-permute-start(bf16[16,2816]{1,0:T(8,128)(2,1)S(1)} %param.8), channel_id=1, source_target_pairs={{0,2},{2,4},{4,0},{6,14},{8,10},{10,12},{12,8},{14,6},{16,18},{18,... | collective-permute-start | bytes 270344 | tf_op jit(solution)/shard_map/cond/branch_8_fun/ppermute | solution.py:277
  14.2 5.8 %collective-permute-start.28 = (bf16[16,2816]{1,0:T(8,128)(2,1)S(1)}, bf16[16,2816]{1,0:T(8,128)(2,1)S(1)}, u32[]{:S(2)}, u32[]{:S(2)}) collective-permute-start(bf16[16,2816]{1,0:T(8,128)(2,1)S(1)} %broadcast_select_fusion.refs_0_), channel_id=1, source_target_pairs={{0,24},{8,16},{16,8},{24,0},{1,25},{9,17},{17,9},{25,1},{2,26},{10... | collective-permute-start | bytes 270344 | tf_op jit(solution)/shard_map/ppermute | solution.py:42
  15.2 4.8 %collective-permute-start.27 = (bf16[16,2816]{1,0:T(8,128)(2,1)S(1)}, bf16[16,2816]{1,0:T(8,128)(2,1)S(1)}, u32[]{:S(2)}, u32[]{:S(2)}) collective-permute-start(bf16[16,2816]{1,0:T(8,128)(2,1)S(1)} %broadcast_select_fusion.refs_0_), channel_id=1, source_target_pairs={{0,16},{8,24},{16,0},{24,8},{1,17},{9,25},{17,1},{25,9},{2,18},{10... | collective-permute-start | bytes 270344 | tf_op jit(solution)/shard_map/ppermute | solution.py:42
  16.9 3.4 %collective-permute-start.26 = (bf16[16,2816]{1,0:T(8,128)(2,1)S(1)}, bf16[16,2816]{1,0:T(8,128)(2,1)S(1)}, u32[]{:S(2)}, u32[]{:S(2)}) collective-permute-start(bf16[16,2816]{1,0:T(8,128)(2,1)S(1)} %broadcast_select_fusion.refs_0_), channel_id=1, source_target_pairs={{0,8},{8,0},{16,24},{24,16},{1,9},{9,1},{17,25},{25,17},{2,10},{10... | collective-permute-start | bytes 270344 | tf_op jit(solution)/shard_map/ppermute | solution.py:42
  20.4 5.7 %collective-permute-start.29 = (bf16[64,2048]{1,0:T(8,128)(2,1)S(1)}, bf16[64,2048]{1,0:T(8,128)(2,1)S(1)}, u32[]{:S(2)}, u32[]{:S(2)}) collective-permute-start(bf16[64,2048]{1,0:T(8,128)(2,1)S(1)} %get-tuple-element.86.refs_1_), channel_id=1, source_target_pairs={{0,1},{1,0},{2,3},{3,2},{4,5},{5,4},{6,7},{7,6},{8,9},{9,8},{10,11... | collective-permute-start | bytes 786440 | tf_op jit(solution)/shard_map/ppermute | solution.py:42

commit v5 on v4

--- a/solution.py
+++ b/solution.py
@@ -178,18 +178,18 @@
     flipped[...] = (rows_b * ADAPTER_SCALE).T.astype(BF16)
 
 
-def merge_kernel(k, width, *refs):
+def merge_kernel(k, rows, *refs):
     panel, rows_a, flipped = refs[:3]
-    out, tiles, sems = refs[-3:]
+    out, tile, sems = refs[-3:]
     cols = rows_a.shape[1]
-    base = (lax.axis_index("tensor") ^ k) * cols
+    columns = pl.ds(pl.multiple_of((lax.axis_index("tensor") ^ k) * cols, cols), cols)
     copies = []
-    for step in range(cols // width):
-        span = slice(step * width, (step + 1) * width)
-        columns = pl.ds(pl.multiple_of(base + step * width, width), width)
-        increment = jnp.dot(flipped[...], rows_a[:, span], preferred_element_type=F32)
-        tiles[step] = (panel[:, columns].astype(F32) + increment).astype(BF16)
-        copy = pltpu.make_async_copy(tiles.at[step], out.at[0, :, columns], sems.at[step])
+    for step in range(panel.shape[0] // rows):
+        here = slice(step * rows, (step + 1) * rows)
+        increment = jnp.dot(flipped[here, :], rows_a[...], preferred_element_type=F32)
+        tile[here, :] = (panel[here, columns].astype(F32) + increment).astype(BF16)
+        part = pl.ds(step * rows, rows)
+        copy = pltpu.make_async_copy(tile.at[part, :], out.at[0, part, columns], sems.at[step])
         copy.start()
         copies.append(copy)
     for copy in copies:
@@ -329,18 +329,18 @@
     )(*map(held, parts), held(panel))
 
     merged = None
-    width = 512
+    step_rows = 128
     for k in range(n_tensor):
         block = held(rows_a if k == 0 else swap(rows_a, "tensor", n_tensor, k))
         operands = [held(panel), block, held(flipped)] + ([] if merged is None else [merged])
         merged = pl.pallas_call(
-            functools.partial(merge_kernel, k, width),
+            functools.partial(merge_kernel, k, step_rows),
             in_specs=[VMEM] * 3 + [HBM] * (len(operands) - 3),
             out_specs=HBM,
             out_shape=jax.ShapeDtypeStruct(weight.shape, BF16),
             scratch_shapes=[
-                pltpu.VMEM((cols_a // width, panel_shape[0], width), BF16),
-                pltpu.SemaphoreType.DMA((cols_a // width,)),
+                pltpu.VMEM((panel_shape[0], cols_a), BF16),
+                pltpu.SemaphoreType.DMA((panel_shape[0] // step_rows,)),
             ],
             input_output_aliases={} if merged is None else {3: 0},
             compiler_params=PARAMS,

time: 28.4 us -> 27.5 us (0.968)
  waiting for transfers between devices: 6.09 us -> 5.08 us
    ppermute x1, waiting for transfers between devices: 2.93 us -> 1.92 us  [branch(): mine = lax.ppermute(send, ('dp', 'expert'), pairs) if moves else send]
  transfers between devices with their start and end apart: 8 -> 8, of which waited for: 5 -> 5; matrix products, arithmetic and copies ran while one was open for 0% -> 0% of each run, Pallas kernels for 22% -> 23%
where the time goes in v5:
time: 27.5 us; the launch traced here: 27.2 us
  starting transfers between devices  11.6 us (42%)
  Pallas kernels  9.75 us (35%)
  waiting for transfers between devices  5.08 us (18%)
  between operations  0.72 us (3%)
    ppermute x7, starting transfers between devices, swap(): return lax.ppermute(x, axis, [(i, i ^ k) for i in range(n)])  9.92 us
    pallas_call x2, Pallas kernels, per_device(): pl.pallas_call(functools.partial(merge_kernel, k, step_rows), in_specs=[V...  3.98 us
    ppermute x7, waiting for transfers between devices, swap(): return lax.ppermute(x, axis, [(i, i ^ k) for i in range(n)])  3.16 us
    pallas_call x1, Pallas kernels, per_device(): pl.pallas_call(functools.partial(state_kernel, n_dp - 1, cols_a), in_spec...  3.04 us
    ppermute x1, waiting for transfers between devices, branch(): mine = lax.ppermute(send, ('dp', 'expert'), pairs) if moves else send  1.92 us
    ppermute x1, starting transfers between devices, branch(): mine = lax.ppermute(send, ('dp', 'expert'), pairs) if moves else send  1.68 us
    pallas_call x1, Pallas kernels, per_device(): pl.pallas_call(functools.partial(load_kernel, ranks, cols_a), in_specs=[H...  1.25 us
    pallas_call x1, Pallas kernels, per_device(): pl.pallas_call(functools.partial(pack_kernel, n_dp, ranks, cols_a), in_sp...  1.16 us
  transfers between devices with their start and end apart: 8, of which 5 were waited for; matrix products, arithmetic and copies ran while one was open for 0% of the time, Pallas kernels for 23%

profile of v5, /device:TPU:1, one launch (start us, length us, event | category | flops | bytes accessed | tf_op | source)
XLA Modules:
  0.0 27.2 jit_solution(14486611045634953336)
XLA Ops:
  0.6 1.2 %pack.1 = (bf16[16,2816]{1,0:T(8,128)(2,1)S(1)}, bf16[16,2816]{1,0:T(8,128)(2,1)S(1)}, bf16[16,2816]{1,0:T(8,128)(2,1)S(1)}) custom-call(f32[1,1,64,2048]{3,2,1,0:T(8,128)} %grad_a.1, f32[1,1,64,768]{3,2,1,0:T(8,128)} %grad_b.1), custom_call_target="tpu_custom_call" | custom-call | tf_op jit(solution)/shard_map/pack/pallas_call | solution.py:218
  1.8 3.1 %collective-permute-start.23 = (bf16[16,2816]{1,0:T(8,128)(2,1)S(1)}, bf16[16,2816]{1,0:T(8,128)(2,1)S(1)}, u32[]{:S(2)}, u32[]{:S(2)}) collective-permute-start(bf16[16,2816]{1,0:T(8,128)(2,1)S(1)} %get-tuple-element.80), channel_id=1, source_target_pairs={{0,24},{8,16},{16,8},{24,0},{1,25},{9,17},{17,9},{25,1},{2,26},{10... | collective-permute-start | bytes 270344 | tf_op jit(solution)/shard_map/ppermute | solution.py:42
  4.9 0.2 collective-permute-start.24
  5.1 0.1 collective-permute-start.25
  5.2 1.3 %load.1 = (f32[16,2816]{1,0:T(8,128)S(1)}, f32[16,2816]{1,0:T(8,128)S(1)}, f32[16,2816]{1,0:T(8,128)S(1)}, f32[16,2816]{1,0:T(8,128)S(1)}, s32[1]{0:T(128)S(4)}, /*index=5*/s32[1]{0:T(128)S(4)}) custom-call(s32[4]{0:T(128)} %slots_in.1, f32[1,1,64,2048]{3,2,1,0:T(8,128)} %grad_a.1, f32[1,1,64,768]{3,2,1,0:T(8,128)} %grad_b.1, f32[1,16,2048]{2,1,0:T(8,128)} %refs_2_.1, ...), custom_call_target="tpu_custom_call" | custom-call | bytes 720896 | tf_op jit(solution)/shard_map/load/pallas_call | solution.py:232
  6.5 0.7 %collective-permute-done.23.refs_4_ = bf16[16,2816]{1,0:T(8,128)(2,1)S(1)} collective-permute-done((bf16[16,2816]{1,0:T(8,128)(2,1)S(1)}, bf16[16,2816]{1,0:T(8,128)(2,1)S(1)}, u32[]{:S(2)}, u32[]{:S(2)}) %collective-permute-start.23) | collective-permute-done | bytes 90144 | tf_op jit(solution)/shard_map/ppermute | solution.py:42
  7.2 1.7 %collective-permute-done.24.refs_5_ = bf16[16,2816]{1,0:T(8,128)(2,1)S(1)} collective-permute-done((bf16[16,2816]{1,0:T(8,128)(2,1)S(1)}, bf16[16,2816]{1,0:T(8,128)(2,1)S(1)}, u32[]{:S(2)}, u32[]{:S(2)}) %collective-permute-start.24) | collective-permute-done | bytes 90144 | tf_op jit(solution)/shard_map/ppermute | solution.py:42
  8.9 0.5 %collective-permute-done.25.refs_6_ = bf16[16,2816]{1,0:T(8,128)(2,1)S(1)} collective-permute-done((bf16[16,2816]{1,0:T(8,128)(2,1)S(1)}, bf16[16,2816]{1,0:T(8,128)(2,1)S(1)}, u32[]{:S(2)}, u32[]{:S(2)}) %collective-permute-start.25) | collective-permute-done | bytes 90144 | tf_op jit(solution)/shard_map/ppermute | solution.py:42
  9.4 0.2 send.1
  9.6 3.7 %conditional.1 = (bf16[16,2816]{1,0:T(8,128)(2,1)S(1)}) conditional(s32[]{:T(128)} %bitcast.1, bf16[16,2816]{1,0:T(8,128)(2,1)S(1)} %send.1, bf16[16,2816]{1,0:T(8,128)(2,1)S(1)} %send.1, bf16[16,2816]{1,0:T(8,128)(2,1)S(1)} %send.1, bf16[16,2816]{1,0:T(8,128)(2,1)S(1)} %send.1, ...), branch_computations={%region_0.0_spmd, %region_1.0_spmd, %region_2.0_spmd, %region_3.0_... | conditional | bytes 360496 | solution.py:291
  9.7 1.7 %collective-permute-start.4 = (bf16[16,2816]{1,0:T(8,128)(2,1)S(1)}, bf16[16,2816]{1,0:T(8,128)(2,1)S(1)}, u32[]{:S(2)}, u32[]{:S(2)}) collective-permute-start(bf16[16,2816]{1,0:T(8,128)(2,1)S(1)} %param.5), channel_id=1, source_target_pairs={{0,8},{2,6},{4,12},{6,2},{8,0},{10,14},{12,4},{14,10},{16,24},{18,... | collective-permute-start | bytes 270344 | tf_op jit(solution)/shard_map/cond/branch_5_fun/ppermute | solution.py:277
  11.3 1.9 %collective-permute-done.4.piece = bf16[16,2816]{1,0:T(8,128)(2,1)S(1)} collective-permute-done((bf16[16,2816]{1,0:T(8,128)(2,1)S(1)}, bf16[16,2816]{1,0:T(8,128)(2,1)S(1)}, u32[]{:S(2)}, u32[]{:S(2)}) %collective-permute-start.4) | collective-permute-done | bytes 90144 | tf_op jit(solution)/shard_map/cond/branch_5_fun/ppermute | solution.py:277
  13.3 1.3 %collective-permute-start.28 = (bf16[16,2816]{1,0:T(8,128)(2,1)S(1)}, bf16[16,2816]{1,0:T(8,128)(2,1)S(1)}, u32[]{:S(2)}, u32[]{:S(2)}) collective-permute-start(bf16[16,2816]{1,0:T(8,128)(2,1)S(1)} %broadcast_select_fusion.refs_0_), channel_id=1, source_target_pairs={{0,24},{8,16},{16,8},{24,0},{1,25},{9,17},{17,9},{25,1},{2,26},{10... | collective-permute-start | bytes 270344 | tf_op jit(solution)/shard_map/ppermute | solution.py:42
  14.6 1.4 %collective-permute-start.27 = (bf16[16,2816]{1,0:T(8,128)(2,1)S(1)}, bf16[16,2816]{1,0:T(8,128)(2,1)S(1)}, u32[]{:S(2)}, u32[]{:S(2)}) collective-permute-start(bf16[16,2816]{1,0:T(8,128)(2,1)S(1)} %broadcast_select_fusion.refs_0_), channel_id=1, source_target_pairs={{0,16},{8,24},{16,0},{24,8},{1,17},{9,25},{17,1},{25,9},{2,18},{10... | collective-permute-start | bytes 270344 | tf_op jit(solution)/shard_map/ppermute | solution.py:42
  16.0 0.1 collective-permute-start.26
  16.1 3.0 %state.1 = (f32[1,16,2048]{2,1,0:T(8,128)}, f32[1,16,768]{2,1,0:T(8,128)}, f32[1,16,2048]{2,1,0:T(8,128)}, f32[1,16,768]{2,1,0:T(8,128)}, f32[1,16,2048]{2,1,0:T...) custom-call(bf16[1,768,4096]{2,1,0:T(8,128)(2,1)} %weight.1, f32[16,2816]{1,0:T(8,128)S(1)} %get-tuple-element.76.refs_0_, ...), custom_call_target="tpu_custom_call" | custom-call | bytes 12582912 | tf_op jit(solution)/shard_map/state/pallas_call | solution.py:304
  19.1 0.0 collective-permute-done.28.refs_3_
  19.1 0.0 collective-permute-done.27.refs_2_
  19.2 0.2 collective-permute-done.26.refs_1_
  19.4 0.1 join.1
  19.5 3.7 %collective-permute-start.29 = (bf16[64,2048]{1,0:T(8,128)(2,1)S(1)}, bf16[64,2048]{1,0:T(8,128)(2,1)S(1)}, u32[]{:S(2)}, u32[]{:S(2)}) collective-permute-start(bf16[64,2048]{1,0:T(8,128)(2,1)S(1)} %get-tuple-element.86.refs_1_), channel_id=1, source_target_pairs={{0,1},{1,0},{2,3},{3,2},{4,5},{5,4},{6,7},{7,6},{8,9},{9,8},{10,11... | collective-permute-start | bytes 786440 | tf_op jit(solution)/shard_map/ppermute | solution.py:42
  23.2 2.0 %merge0.1.refs_3_ = bf16[1,768,4096]{2,1,0:T(8,128)(2,1)} custom-call(bf16[768,4096]{1,0:T(8,128)(2,1)S(1)} %get-tuple-element.85.refs_0_, bf16[64,2048]{1,0:T(8,128)(2,1)S(1)} %get-tuple-element.86.refs_1_, bf16[768,64]{1,0:T(8,128)(2,1)S(1)} %get-tuple-element.87.refs_2_), custom_call_target="tpu_custom_call" | custom-call | flops 201326592 | bytes 3145728 | tf_op jit(solution)/shard_map/merge0/pallas_call | solution.py:336
  25.2 0.0 collective-permute-done.29.refs_1_
  25.2 2.0 %merge1.1 = bf16[1,768,4096]{2,1,0:T(8,128)(2,1)} custom-call(bf16[768,4096]{1,0:T(8,128)(2,1)S(1)} %get-tuple-element.85.refs_0_, bf16[64,2048]{1,0:T(8,128)(2,1)S(1)} %collective-permute-done.29.refs_1_, bf16[768,64]{1,0:T(8,128)(2,1)S(1)} %get-tuple-element.87.refs_2_, bf16[1,768,4096]{2,1,0:T(8,128)(2,1)} %merge0.1.refs_3_), custom_call_target="tpu_custom_call", output_to_operand_aliasing={{}: (3, {})} | custom-call | flops 201326592 | bytes 3145728 | tf_op jit(solution)/shard_map/merge1/pallas_call | solution.py:336
  (2 shorter events, 0.0 us)
Async XLA Ops:
  1.8 5.4 %collective-permute-start.23 = (bf16[16,2816]{1,0:T(8,128)(2,1)S(1)}, bf16[16,2816]{1,0:T(8,128)(2,1)S(1)}, u32[]{:S(2)}, u32[]{:S(2)}) collective-permute-start(bf16[16,2816]{1,0:T(8,128)(2,1)S(1)} %get-tuple-element.80), channel_id=1, source_target_pairs={{0,24},{8,16},{16,8},{24,0},{1,25},{9,17},{17,9},{25,1},{2,26},{10... | collective-permute-start | bytes 270344 | tf_op jit(solution)/shard_map/ppermute | solution.py:42
  4.9 4.1 %collective-permute-start.24 = (bf16[16,2816]{1,0:T(8,128)(2,1)S(1)}, bf16[16,2816]{1,0:T(8,128)(2,1)S(1)}, u32[]{:S(2)}, u32[]{:S(2)}) collective-permute-start(bf16[16,2816]{1,0:T(8,128)(2,1)S(1)} %get-tuple-element.81), channel_id=1, source_target_pairs={{0,16},{8,24},{16,0},{24,8},{1,17},{9,25},{17,1},{25,9},{2,18},{10... | collective-permute-start | bytes 270344 | tf_op jit(solution)/shard_map/ppermute | solution.py:42
  5.1 4.3 %collective-permute-start.25 = (bf16[16,2816]{1,0:T(8,128)(2,1)S(1)}, bf16[16,2816]{1,0:T(8,128)(2,1)S(1)}, u32[]{:S(2)}, u32[]{:S(2)}) collective-permute-start(bf16[16,2816]{1,0:T(8,128)(2,1)S(1)} %get-tuple-element.82), channel_id=1, source_target_pairs={{0,8},{8,0},{16,24},{24,16},{1,9},{9,1},{17,25},{25,17},{2,10},{10... | collective-permute-start | bytes 270344 | tf_op jit(solution)/shard_map/ppermute | solution.py:42
  9.7 3.6 %collective-permute-start.4 = (bf16[16,2816]{1,0:T(8,128)(2,1)S(1)}, bf16[16,2816]{1,0:T(8,128)(2,1)S(1)}, u32[]{:S(2)}, u32[]{:S(2)}) collective-permute-start(bf16[16,2816]{1,0:T(8,128)(2,1)S(1)} %param.5), channel_id=1, source_target_pairs={{0,8},{2,6},{4,12},{6,2},{8,0},{10,14},{12,4},{14,10},{16,24},{18,... | collective-permute-start | bytes 270344 | tf_op jit(solution)/shard_map/cond/branch_5_fun/ppermute | solution.py:277
  13.3 5.8 %collective-permute-start.28 = (bf16[16,2816]{1,0:T(8,128)(2,1)S(1)}, bf16[16,2816]{1,0:T(8,128)(2,1)S(1)}, u32[]{:S(2)}, u32[]{:S(2)}) collective-permute-start(bf16[16,2816]{1,0:T(8,128)(2,1)S(1)} %broadcast_select_fusion.refs_0_), channel_id=1, source_target_pairs={{0,24},{8,16},{16,8},{24,0},{1,25},{9,17},{17,9},{25,1},{2,26},{10... | collective-permute-start | bytes 270344 | tf_op jit(solution)/shard_map/ppermute | solution.py:42
  14.6 4.5 %collective-permute-start.27 = (bf16[16,2816]{1,0:T(8,128)(2,1)S(1)}, bf16[16,2816]{1,0:T(8,128)(2,1)S(1)}, u32[]{:S(2)}, u32[]{:S(2)}) collective-permute-start(bf16[16,2816]{1,0:T(8,128)(2,1)S(1)} %broadcast_select_fusion.refs_0_), channel_id=1, source_target_pairs={{0,16},{8,24},{16,0},{24,8},{1,17},{9,25},{17,1},{25,9},{2,18},{10... | collective-permute-start | bytes 270344 | tf_op jit(solution)/shard_map/ppermute | solution.py:42
  16.0 3.4 %collective-permute-start.26 = (bf16[16,2816]{1,0:T(8,128)(2,1)S(1)}, bf16[16,2816]{1,0:T(8,128)(2,1)S(1)}, u32[]{:S(2)}, u32[]{:S(2)}) collective-permute-start(bf16[16,2816]{1,0:T(8,128)(2,1)S(1)} %broadcast_select_fusion.refs_0_), channel_id=1, source_target_pairs={{0,8},{8,0},{16,24},{24,16},{1,9},{9,1},{17,25},{25,17},{2,10},{10... | collective-permute-start | bytes 270344 | tf_op jit(solution)/shard_map/ppermute | solution.py:42
  19.5 5.7 %collective-permute-start.29 = (bf16[64,2048]{1,0:T(8,128)(2,1)S(1)}, bf16[64,2048]{1,0:T(8,128)(2,1)S(1)}, u32[]{:S(2)}, u32[]{:S(2)}) collective-permute-start(bf16[64,2048]{1,0:T(8,128)(2,1)S(1)} %get-tuple-element.86.refs_1_), channel_id=1, source_target_pairs={{0,1},{1,0},{2,3},{3,2},{4,5},{5,4},{6,7},{7,6},{8,9},{9,8},{10,11... | collective-permute-start | bytes 786440 | tf_op jit(solution)/shard_map/ppermute | solution.py:42

commit v6 on v5

--- a/solution.py
+++ b/solution.py
@@ -266,15 +266,17 @@
     )(*state, *got)
 
     def move(slots):
-        pairs = [
-            (i * n_expert + expert, (i if expert != slot else i ^ 1) * n_expert + slot)
-            for i in range(n_dp)
-            for expert, slot in enumerate(slots)
-        ]
+        pairs = []
+        for i, (expert, slot), j in itertools.product(
+            range(n_dp), enumerate(slots), range(n_tensor)
+        ):
+            source = (i * n_expert + expert) * n_tensor + j
+            partner = j if expert != slot else (j + 1) % n_tensor
+            pairs.append((source, (i * n_expert + slot) * n_tensor + partner))
         moves = any(expert != slot for expert, slot in enumerate(slots))
 
         def branch(send):
-            mine = lax.ppermute(send, ("dp", "expert"), pairs) if moves else send
+            mine = lax.ppermute(send, ("dp", "expert", "tensor"), pairs) if moves else send
             return pl.pallas_call(
                 keep_kernel,
                 in_specs=[VMEM],

time: 27.5 us -> 28 us (1.018)
  the two profiles are of different devices: /device:TPU:1 before, /device:TPU:25 now
where the time goes in v6:
time: 28 us; the launch traced here: 28.2 us
  Pallas kernels  9.75 us (35%)
  starting transfers between devices  9.24 us (33%)
  waiting for transfers between devices  8.39 us (30%)
  between operations  0.72 us (3%)
    ppermute x7, starting transfers between devices, swap(): return lax.ppermute(x, axis, [(i, i ^ k) for i in range(n)])  9.13 us
    ppermute x1, waiting for transfers between devices, branch(): lax.ppermute(send, ('dp', 'expert', 'tensor'), pairs)  5.12 us
    pallas_call x2, Pallas kernels, per_device(): pl.pallas_call(functools.partial(merge_kernel, k, step_rows), in_specs=[V...  3.98 us
    ppermute x7, waiting for transfers between devices, swap(): return lax.ppermute(x, axis, [(i, i ^ k) for i in range(n)])  3.28 us
    pallas_call x1, Pallas kernels, per_device(): pl.pallas_call(functools.partial(state_kernel, n_dp - 1, cols_a), in_spec...  3.04 us
    pallas_call x1, Pallas kernels, per_device(): pl.pallas_call(functools.partial(load_kernel, ranks, cols_a), in_specs=[H...  1.25 us
    pallas_call x1, Pallas kernels, per_device(): pl.pallas_call(functools.partial(pack_kernel, n_dp, ranks, cols_a), in_sp...  1.16 us
  transfers between devices with their start and end apart: 8, of which 4 were waited for; matrix products, arithmetic and copies ran while one was open for 0% of the time, Pallas kernels for 22%

profile of v6, /device:TPU:25, one launch (start us, length us, event | category | flops | bytes accessed | tf_op | source)
XLA Modules:
  0.0 28.2 jit_solution(7170767267689965266)
XLA Ops:
  0.6 1.2 %pack.1 = (bf16[16,2816]{1,0:T(8,128)(2,1)S(1)}, bf16[16,2816]{1,0:T(8,128)(2,1)S(1)}, bf16[16,2816]{1,0:T(8,128)(2,1)S(1)}) custom-call(f32[1,1,64,2048]{3,2,1,0:T(8,128)} %grad_a.1, f32[1,1,64,768]{3,2,1,0:T(8,128)} %grad_b.1), custom_call_target="tpu_custom_call" | custom-call | tf_op jit(solution)/shard_map/pack/pallas_call | solution.py:218
  1.8 2.2 %collective-permute-start.23 = (bf16[16,2816]{1,0:T(8,128)(2,1)S(1)}, bf16[16,2816]{1,0:T(8,128)(2,1)S(1)}, u32[]{:S(2)}, u32[]{:S(2)}) collective-permute-start(bf16[16,2816]{1,0:T(8,128)(2,1)S(1)} %get-tuple-element.80), channel_id=1, source_target_pairs={{0,24},{8,16},{16,8},{24,0},{1,25},{9,17},{17,9},{25,1},{2,26},{10... | collective-permute-start | bytes 270344 | tf_op jit(solution)/shard_map/ppermute | solution.py:42
  4.0 0.2 collective-permute-start.24
  4.3 0.3 collective-permute-start.25
  4.5 1.3 %load.1 = (f32[16,2816]{1,0:T(8,128)S(1)}, f32[16,2816]{1,0:T(8,128)S(1)}, f32[16,2816]{1,0:T(8,128)S(1)}, f32[16,2816]{1,0:T(8,128)S(1)}, s32[1]{0:T(128)S(4)}, /*index=5*/s32[1]{0:T(128)S(4)}) custom-call(s32[4]{0:T(128)} %slots_in.1, f32[1,1,64,2048]{3,2,1,0:T(8,128)} %grad_a.1, f32[1,1,64,768]{3,2,1,0:T(8,128)} %grad_b.1, f32[1,16,2048]{2,1,0:T(8,128)} %refs_2_.1, ...), custom_call_target="tpu_custom_call" | custom-call | bytes 720896 | tf_op jit(solution)/shard_map/load/pallas_call | solution.py:232
  5.8 0.4 %collective-permute-done.23.refs_4_ = bf16[16,2816]{1,0:T(8,128)(2,1)S(1)} collective-permute-done((bf16[16,2816]{1,0:T(8,128)(2,1)S(1)}, bf16[16,2816]{1,0:T(8,128)(2,1)S(1)}, u32[]{:S(2)}, u32[]{:S(2)}) %collective-permute-start.23) | collective-permute-done | bytes 90144 | tf_op jit(solution)/shard_map/ppermute | solution.py:42
  6.1 2.7 %collective-permute-done.24.refs_5_ = bf16[16,2816]{1,0:T(8,128)(2,1)S(1)} collective-permute-done((bf16[16,2816]{1,0:T(8,128)(2,1)S(1)}, bf16[16,2816]{1,0:T(8,128)(2,1)S(1)}, u32[]{:S(2)}, u32[]{:S(2)}) %collective-permute-start.24) | collective-permute-done | bytes 90144 | tf_op jit(solution)/shard_map/ppermute | solution.py:42
  8.9 0.0 collective-permute-done.25.refs_6_
  8.9 0.2 send.1
  9.0 5.3 %conditional.1 = (bf16[16,2816]{1,0:T(8,128)(2,1)S(1)}) conditional(s32[]{:T(128)} %bitcast.1, bf16[16,2816]{1,0:T(8,128)(2,1)S(1)} %send.1, bf16[16,2816]{1,0:T(8,128)(2,1)S(1)} %send.1, bf16[16,2816]{1,0:T(8,128)(2,1)S(1)} %send.1, bf16[16,2816]{1,0:T(8,128)(2,1)S(1)} %send.1, ...), branch_computations={%region_0.0_spmd, %region_1.0_spmd, %region_2.0_spmd, %region_3.0_... | conditional | bytes 360496 | solution.py:293
  9.1 0.1 collective-permute-start.18
  9.2 5.1 %collective-permute-done.18.piece = bf16[16,2816]{1,0:T(8,128)(2,1)S(1)} collective-permute-done((bf16[16,2816]{1,0:T(8,128)(2,1)S(1)}, bf16[16,2816]{1,0:T(8,128)(2,1)S(1)}, u32[]{:S(2)}, u32[]{:S(2)}) %collective-permute-start.18) | collective-permute-done | bytes 90144 | tf_op jit(solution)/shard_map/cond/branch_19_fun/ppermute | solution.py:279
  14.4 0.9 %collective-permute-start.28 = (bf16[16,2816]{1,0:T(8,128)(2,1)S(1)}, bf16[16,2816]{1,0:T(8,128)(2,1)S(1)}, u32[]{:S(2)}, u32[]{:S(2)}) collective-permute-start(bf16[16,2816]{1,0:T(8,128)(2,1)S(1)} %broadcast_select_fusion.refs_0_), channel_id=1, source_target_pairs={{0,24},{8,16},{16,8},{24,0},{1,25},{9,17},{17,9},{25,1},{2,26},{10... | collective-permute-start | bytes 270344 | tf_op jit(solution)/shard_map/ppermute | solution.py:42
  15.3 1.6 %collective-permute-start.27 = (bf16[16,2816]{1,0:T(8,128)(2,1)S(1)}, bf16[16,2816]{1,0:T(8,128)(2,1)S(1)}, u32[]{:S(2)}, u32[]{:S(2)}) collective-permute-start(bf16[16,2816]{1,0:T(8,128)(2,1)S(1)} %broadcast_select_fusion.refs_0_), channel_id=1, source_target_pairs={{0,16},{8,24},{16,0},{24,8},{1,17},{9,25},{17,1},{25,9},{2,18},{10... | collective-permute-start | bytes 270344 | tf_op jit(solution)/shard_map/ppermute | solution.py:42
  17.0 0.1 collective-permute-start.26
  17.1 3.0 %state.1 = (f32[1,16,2048]{2,1,0:T(8,128)}, f32[1,16,768]{2,1,0:T(8,128)}, f32[1,16,2048]{2,1,0:T(8,128)}, f32[1,16,768]{2,1,0:T(8,128)}, f32[1,16,2048]{2,1,0:T...) custom-call(bf16[1,768,4096]{2,1,0:T(8,128)(2,1)} %weight.1, f32[16,2816]{1,0:T(8,128)S(1)} %get-tuple-element.76.refs_0_, ...), custom_call_target="tpu_custom_call" | custom-call | bytes 12582912 | tf_op jit(solution)/shard_map/state/pallas_call | solution.py:306
  20.1 0.0 collective-permute-done.28.refs_3_
  20.1 0.0 collective-permute-done.27.refs_2_
  20.1 0.2 collective-permute-done.26.refs_1_
  20.3 0.1 join.1
  20.5 3.7 %collective-permute-start.29 = (bf16[64,2048]{1,0:T(8,128)(2,1)S(1)}, bf16[64,2048]{1,0:T(8,128)(2,1)S(1)}, u32[]{:S(2)}, u32[]{:S(2)}) collective-permute-start(bf16[64,2048]{1,0:T(8,128)(2,1)S(1)} %get-tuple-element.86.refs_1_), channel_id=1, source_target_pairs={{0,1},{1,0},{2,3},{3,2},{4,5},{5,4},{6,7},{7,6},{8,9},{9,8},{10,11... | collective-permute-start | bytes 786440 | tf_op jit(solution)/shard_map/ppermute | solution.py:42
  24.2 2.0 %merge0.1.refs_3_ = bf16[1,768,4096]{2,1,0:T(8,128)(2,1)} custom-call(bf16[768,4096]{1,0:T(8,128)(2,1)S(1)} %get-tuple-element.85.refs_0_, bf16[64,2048]{1,0:T(8,128)(2,1)S(1)} %get-tuple-element.86.refs_1_, bf16[768,64]{1,0:T(8,128)(2,1)S(1)} %get-tuple-element.87.refs_2_), custom_call_target="tpu_custom_call" | custom-call | flops 201326592 | bytes 3145728 | tf_op jit(solution)/shard_map/merge0/pallas_call | solution.py:338
  26.2 0.0 collective-permute-done.29.refs_1_
  26.2 2.0 %merge1.1 = bf16[1,768,4096]{2,1,0:T(8,128)(2,1)} custom-call(bf16[768,4096]{1,0:T(8,128)(2,1)S(1)} %get-tuple-element.85.refs_0_, bf16[64,2048]{1,0:T(8,128)(2,1)S(1)} %collective-permute-done.29.refs_1_, bf16[768,64]{1,0:T(8,128)(2,1)S(1)} %get-tuple-element.87.refs_2_, bf16[1,768,4096]{2,1,0:T(8,128)(2,1)} %merge0.1.refs_3_), custom_call_target="tpu_custom_call", output_to_operand_aliasing={{}: (3, {})} | custom-call | flops 201326592 | bytes 3145728 | tf_op jit(solution)/shard_map/merge1/pallas_call | solution.py:338
  (2 shorter events, 0.0 us)
Async XLA Ops:
  1.8 4.3 %collective-permute-start.23 = (bf16[16,2816]{1,0:T(8,128)(2,1)S(1)}, bf16[16,2816]{1,0:T(8,128)(2,1)S(1)}, u32[]{:S(2)}, u32[]{:S(2)}) collective-permute-start(bf16[16,2816]{1,0:T(8,128)(2,1)S(1)} %get-tuple-element.80), channel_id=1, source_target_pairs={{0,24},{8,16},{16,8},{24,0},{1,25},{9,17},{17,9},{25,1},{2,26},{10... | collective-permute-start | bytes 270344 | tf_op jit(solution)/shard_map/ppermute | solution.py:42
  4.0 4.8 %collective-permute-start.24 = (bf16[16,2816]{1,0:T(8,128)(2,1)S(1)}, bf16[16,2816]{1,0:T(8,128)(2,1)S(1)}, u32[]{:S(2)}, u32[]{:S(2)}) collective-permute-start(bf16[16,2816]{1,0:T(8,128)(2,1)S(1)} %get-tuple-element.81), channel_id=1, source_target_pairs={{0,16},{8,24},{16,0},{24,8},{1,17},{9,25},{17,1},{25,9},{2,18},{10... | collective-permute-start | bytes 270344 | tf_op jit(solution)/shard_map/ppermute | solution.py:42
  4.3 4.6 %collective-permute-start.25 = (bf16[16,2816]{1,0:T(8,128)(2,1)S(1)}, bf16[16,2816]{1,0:T(8,128)(2,1)S(1)}, u32[]{:S(2)}, u32[]{:S(2)}) collective-permute-start(bf16[16,2816]{1,0:T(8,128)(2,1)S(1)} %get-tuple-element.82), channel_id=1, source_target_pairs={{0,8},{8,0},{16,24},{24,16},{1,9},{9,1},{17,25},{25,17},{2,10},{10... | collective-permute-start | bytes 270344 | tf_op jit(solution)/shard_map/ppermute | solution.py:42
  9.1 5.2 %collective-permute-start.18 = (bf16[16,2816]{1,0:T(8,128)(2,1)S(1)}, bf16[16,2816]{1,0:T(8,128)(2,1)S(1)}, u32[]{:S(2)}, u32[]{:S(2)}) collective-permute-start(bf16[16,2816]{1,0:T(8,128)(2,1)S(1)} %param.19), channel_id=1, source_target_pairs={{0,6},{1,7},{2,0},{3,1},{4,5},{5,4},{6,2},{7,3},{8,14},{9,15},{10,... | collective-permute-start | bytes 270344 | tf_op jit(solution)/shard_map/cond/branch_19_fun/ppermute | solution.py:279
  14.4 5.8 %collective-permute-start.28 = (bf16[16,2816]{1,0:T(8,128)(2,1)S(1)}, bf16[16,2816]{1,0:T(8,128)(2,1)S(1)}, u32[]{:S(2)}, u32[]{:S(2)}) collective-permute-start(bf16[16,2816]{1,0:T(8,128)(2,1)S(1)} %broadcast_select_fusion.refs_0_), channel_id=1, source_target_pairs={{0,24},{8,16},{16,8},{24,0},{1,25},{9,17},{17,9},{25,1},{2,26},{10... | collective-permute-start | bytes 270344 | tf_op jit(solution)/shard_map/ppermute | solution.py:42
  15.3 4.8 %collective-permute-start.27 = (bf16[16,2816]{1,0:T(8,128)(2,1)S(1)}, bf16[16,2816]{1,0:T(8,128)(2,1)S(1)}, u32[]{:S(2)}, u32[]{:S(2)}) collective-permute-start(bf16[16,2816]{1,0:T(8,128)(2,1)S(1)} %broadcast_select_fusion.refs_0_), channel_id=1, source_target_pairs={{0,16},{8,24},{16,0},{24,8},{1,17},{9,25},{17,1},{25,9},{2,18},{10... | collective-permute-start | bytes 270344 | tf_op jit(solution)/shard_map/ppermute | solution.py:42
  17.0 3.4 %collective-permute-start.26 = (bf16[16,2816]{1,0:T(8,128)(2,1)S(1)}, bf16[16,2816]{1,0:T(8,128)(2,1)S(1)}, u32[]{:S(2)}, u32[]{:S(2)}) collective-permute-start(bf16[16,2816]{1,0:T(8,128)(2,1)S(1)} %broadcast_select_fusion.refs_0_), channel_id=1, source_target_pairs={{0,8},{8,0},{16,24},{24,16},{1,9},{9,1},{17,25},{25,17},{2,10},{10... | collective-permute-start | bytes 270344 | tf_op jit(solution)/shard_map/ppermute | solution.py:42
  20.5 5.7 %collective-permute-start.29 = (bf16[64,2048]{1,0:T(8,128)(2,1)S(1)}, bf16[64,2048]{1,0:T(8,128)(2,1)S(1)}, u32[]{:S(2)}, u32[]{:S(2)}) collective-permute-start(bf16[64,2048]{1,0:T(8,128)(2,1)S(1)} %get-tuple-element.86.refs_1_), channel_id=1, source_target_pairs={{0,1},{1,0},{2,3},{3,2},{4,5},{5,4},{6,7},{7,6},{8,9},{9,8},{10,11... | collective-permute-start | bytes 786440 | tf_op jit(solution)/shard_map/ppermute | solution.py:42

commit v7 on v6

--- a/solution.py
+++ b/solution.py
@@ -129,6 +129,12 @@
     refs[-1][...] = adam_update(factor[...], moment[...], second[...], total)[0].astype(BF16)
 
 
+def shard_copy(weight, panel, k, sem):
+    cols = panel.shape[1]
+    at = pl.multiple_of((lax.axis_index("tensor") ^ k) * cols, cols)
+    return pltpu.make_async_copy(weight.at[0, :, pl.ds(at, cols)], panel, sem)
+
+
 def state_kernel(n_got, cols_a, weight, *refs):
     ins = refs[: 4 + n_got]
     outs = refs[4 + n_got : 10 + n_got]
@@ -137,7 +143,7 @@
     sems = refs[-1]
     cols_b = ins[0].shape[1] - cols_a
     width = 256 if cols_a % 256 == 0 and cols_b % 256 == 0 else 128
-    load = pltpu.make_async_copy(weight.at[0], panel, sems.at[0])
+    load = shard_copy(weight, panel, 0, sems.at[0])
     load.start()
 
     def some_columns(start, into, at):
@@ -178,22 +184,29 @@
     flipped[...] = (rows_b * ADAPTER_SCALE).T.astype(BF16)
 
 
-def merge_kernel(k, rows, *refs):
+def merge_kernel(k, rows, load_next, *refs):
     panel, rows_a, flipped = refs[:3]
-    out, tile, sems = refs[-3:]
+    tile, sems, load_sem = refs[-3:]
+    out = refs[-5] if load_next else refs[-4]
     cols = rows_a.shape[1]
     columns = pl.ds(pl.multiple_of((lax.axis_index("tensor") ^ k) * cols, cols), cols)
+    load = None
+    if load_next:
+        load = shard_copy(refs[3], refs[-4], k + 1, load_sem.at[0])
+        load.start()
     copies = []
     for step in range(panel.shape[0] // rows):
         here = slice(step * rows, (step + 1) * rows)
         increment = jnp.dot(flipped[here, :], rows_a[...], preferred_element_type=F32)
-        tile[here, :] = (panel[here, columns].astype(F32) + increment).astype(BF16)
+        tile[here, :] = (panel[here, :].astype(F32) + increment).astype(BF16)
         part = pl.ds(step * rows, rows)
         copy = pltpu.make_async_copy(tile.at[part, :], out.at[0, part, columns], sems.at[step])
         copy.start()
         copies.append(copy)
     for copy in copies:
         copy.wait()
+    if load is not None:
+        load.wait()
 
 
 def per_device(
@@ -301,7 +314,7 @@
             mine = jnp.where(wanted == k, swap(send, "expert", n_expert, k), mine)
 
     parts = [mine] + [swap(mine, "dp", n_dp, k) for k in range(1, n_dp)]
-    panel_shape = weight.shape[1:]
+    panel_shape = (weight.shape[1], cols_a)
     shapes = [factor_a.shape, factor_b.shape] * 3
     *new, panel = pl.pallas_call(
         functools.partial(state_kernel, n_dp - 1, cols_a),
@@ -334,23 +347,29 @@
     step_rows = 128
     for k in range(n_tensor):
         block = held(rows_a if k == 0 else swap(rows_a, "tensor", n_tensor, k))
-        operands = [held(panel), block, held(flipped)] + ([] if merged is None else [merged])
-        merged = pl.pallas_call(
-            functools.partial(merge_kernel, k, step_rows),
+        load_next = k < n_tensor - 1
+        operands = [held(panel), block, held(flipped)]
+        operands += [left(weight)] if load_next else []
+        operands += [] if merged is None else [merged]
+        merged, *panels = pl.pallas_call(
+            functools.partial(merge_kernel, k, step_rows, load_next),
             in_specs=[VMEM] * 3 + [HBM] * (len(operands) - 3),
-            out_specs=HBM,
-            out_shape=jax.ShapeDtypeStruct(weight.shape, BF16),
+            out_specs=[HBM] + [VMEM] * load_next,
+            out_shape=[jax.ShapeDtypeStruct(weight.shape, BF16)]
+            + [pltpu.VMEM(panel_shape, BF16)] * load_next,
             scratch_shapes=[
-                pltpu.VMEM((panel_shape[0], cols_a), BF16),
+                pltpu.VMEM(panel_shape, BF16),
                 pltpu.SemaphoreType.DMA((panel_shape[0] // step_rows,)),
+                pltpu.SemaphoreType.DMA((1,)),
             ],
-            input_output_aliases={} if merged is None else {3: 0},
+            input_output_aliases={} if merged is None else {len(operands) - 1: 0},
             compiler_params=PARAMS,
             cost_estimate=estimate(
                 panel_shape[0] * cols_a * 2, 2 * panel_shape[0] * cols_a * ranks * n_dp
             ),
             name=f"merge{k}",
         )(*operands)
+        panel = panels[0] if load_next else None
     return (merged, new_a, new_b, new_moment_a, new_second_a, new_moment_b, new_second_b)
 
 

time: 28 us -> 28.9 us (1.032)
  the two profiles are of different devices: /device:TPU:25 before, /device:TPU:9 now
where the time goes in v7:
time: 28.9 us; the launch traced here: 28.7 us
  starting transfers between devices  11.5 us (40%)
  Pallas kernels  10.2 us (35%)
  waiting for transfers between devices  6.15 us (21%)
  between operations  0.71 us (2%)
    ppermute x7, starting transfers between devices, swap(): return lax.ppermute(x, axis, [(i, i ^ k) for i in range(n)])  9.13 us
    pallas_call x2, Pallas kernels, per_device(): pl.pallas_call(functools.partial(merge_kernel, k, step_rows, load_next),...  5.33 us
    ppermute x7, waiting for transfers between devices, swap(): return lax.ppermute(x, axis, [(i, i ^ k) for i in range(n)])  4.18 us
    ppermute x1, starting transfers between devices, branch(): lax.ppermute(send, ('dp', 'expert', 'tensor'), pairs)  2.37 us
    pallas_call x1, Pallas kernels, per_device(): pl.pallas_call(functools.partial(state_kernel, n_dp - 1, cols_a), in_spec...  2.14 us
    ppermute x1, waiting for transfers between devices, branch(): lax.ppermute(send, ('dp', 'expert', 'tensor'), pairs)  1.97 us
    pallas_call x1, Pallas kernels, per_device(): pl.pallas_call(functools.partial(load_kernel, ranks, cols_a), in_specs=[H...  1.25 us
    pallas_call x1, Pallas kernels, per_device(): pl.pallas_call(functools.partial(pack_kernel, n_dp, ranks, cols_a), in_sp...  1.16 us
  transfers between devices with their start and end apart: 8, of which 5 were waited for; matrix products, arithmetic and copies ran while one was open for 0% of the time, Pallas kernels for 23%

profile of v7, /device:TPU:9, one launch (start us, length us, event | category | flops | bytes accessed | tf_op | source)
XLA Modules:
  0.0 28.7 jit_solution(6979316516031760284)
XLA Ops:
  0.6 1.2 %pack.1 = (bf16[16,2816]{1,0:T(8,128)(2,1)S(1)}, bf16[16,2816]{1,0:T(8,128)(2,1)S(1)}, bf16[16,2816]{1,0:T(8,128)(2,1)S(1)}) custom-call(f32[1,1,64,2048]{3,2,1,0:T(8,128)} %grad_a.1, f32[1,1,64,768]{3,2,1,0:T(8,128)} %grad_b.1), custom_call_target="tpu_custom_call" | custom-call | tf_op jit(solution)/shard_map/pack/pallas_call | solution.py:231
  1.8 2.2 %collective-permute-start.23 = (bf16[16,2816]{1,0:T(8,128)(2,1)S(1)}, bf16[16,2816]{1,0:T(8,128)(2,1)S(1)}, u32[]{:S(2)}, u32[]{:S(2)}) collective-permute-start(bf16[16,2816]{1,0:T(8,128)(2,1)S(1)} %get-tuple-element.82), channel_id=1, source_target_pairs={{0,24},{8,16},{16,8},{24,0},{1,25},{9,17},{17,9},{25,1},{2,26},{10... | collective-permute-start | bytes 270344 | tf_op jit(solution)/shard_map/ppermute | solution.py:42
  4.0 0.2 collective-permute-start.24
  4.3 0.3 collective-permute-start.25
  4.5 1.3 %load.1 = (f32[16,2816]{1,0:T(8,128)S(1)}, f32[16,2816]{1,0:T(8,128)S(1)}, f32[16,2816]{1,0:T(8,128)S(1)}, f32[16,2816]{1,0:T(8,128)S(1)}, s32[1]{0:T(128)S(4)}, /*index=5*/s32[1]{0:T(128)S(4)}) custom-call(s32[4]{0:T(128)} %slots_in.1, f32[1,1,64,2048]{3,2,1,0:T(8,128)} %grad_a.1, f32[1,1,64,768]{3,2,1,0:T(8,128)} %grad_b.1, f32[1,16,2048]{2,1,0:T(8,128)} %refs_2_.1, ...), custom_call_target="tpu_custom_call" | custom-call | bytes 720896 | tf_op jit(solution)/shard_map/load/pallas_call | solution.py:245
  5.8 0.4 %collective-permute-done.23.refs_4_ = bf16[16,2816]{1,0:T(8,128)(2,1)S(1)} collective-permute-done((bf16[16,2816]{1,0:T(8,128)(2,1)S(1)}, bf16[16,2816]{1,0:T(8,128)(2,1)S(1)}, u32[]{:S(2)}, u32[]{:S(2)}) %collective-permute-start.23) | collective-permute-done | bytes 90144 | tf_op jit(solution)/shard_map/ppermute | solution.py:42
  6.1 2.7 %collective-permute-done.24.refs_5_ = bf16[16,2816]{1,0:T(8,128)(2,1)S(1)} collective-permute-done((bf16[16,2816]{1,0:T(8,128)(2,1)S(1)}, bf16[16,2816]{1,0:T(8,128)(2,1)S(1)}, u32[]{:S(2)}, u32[]{:S(2)}) %collective-permute-start.24) | collective-permute-done | bytes 90144 | tf_op jit(solution)/shard_map/ppermute | solution.py:42
  8.9 0.0 collective-permute-done.25.refs_6_
  8.9 0.2 send.1
  9.0 4.4 %conditional.1 = (bf16[16,2816]{1,0:T(8,128)(2,1)S(1)}) conditional(s32[]{:T(128)} %bitcast.1, bf16[16,2816]{1,0:T(8,128)(2,1)S(1)} %send.1, bf16[16,2816]{1,0:T(8,128)(2,1)S(1)} %send.1, bf16[16,2816]{1,0:T(8,128)(2,1)S(1)} %send.1, bf16[16,2816]{1,0:T(8,128)(2,1)S(1)} %send.1, ...), branch_computations={%region_0.0_spmd, %region_1.0_spmd, %region_2.0_spmd, %region_3.0_... | conditional | bytes 360496 | solution.py:306
  9.1 2.4 %collective-permute-start.4 = (bf16[16,2816]{1,0:T(8,128)(2,1)S(1)}, bf16[16,2816]{1,0:T(8,128)(2,1)S(1)}, u32[]{:S(2)}, u32[]{:S(2)}) collective-permute-start(bf16[16,2816]{1,0:T(8,128)(2,1)S(1)} %param.5), channel_id=1, source_target_pairs={{0,1},{1,0},{2,6},{3,7},{4,5},{5,4},{6,2},{7,3},{8,9},{9,8},{10,14... | collective-permute-start | bytes 270344 | tf_op jit(solution)/shard_map/cond/branch_5_fun/ppermute | solution.py:292
  11.5 2.0 %collective-permute-done.4.piece = bf16[16,2816]{1,0:T(8,128)(2,1)S(1)} collective-permute-done((bf16[16,2816]{1,0:T(8,128)(2,1)S(1)}, bf16[16,2816]{1,0:T(8,128)(2,1)S(1)}, u32[]{:S(2)}, u32[]{:S(2)}) %collective-permute-start.4) | collective-permute-done | bytes 90144 | tf_op jit(solution)/shard_map/cond/branch_5_fun/ppermute | solution.py:292
  13.5 0.9 %collective-permute-start.28 = (bf16[16,2816]{1,0:T(8,128)(2,1)S(1)}, bf16[16,2816]{1,0:T(8,128)(2,1)S(1)}, u32[]{:S(2)}, u32[]{:S(2)}) collective-permute-start(bf16[16,2816]{1,0:T(8,128)(2,1)S(1)} %broadcast_select_fusion.refs_0_), channel_id=1, source_target_pairs={{0,24},{8,16},{16,8},{24,0},{1,25},{9,17},{17,9},{25,1},{2,26},{10... | collective-permute-start | bytes 270344 | tf_op jit(solution)/shard_map/ppermute | solution.py:42
  14.4 1.6 %collective-permute-start.27 = (bf16[16,2816]{1,0:T(8,128)(2,1)S(1)}, bf16[16,2816]{1,0:T(8,128)(2,1)S(1)}, u32[]{:S(2)}, u32[]{:S(2)}) collective-permute-start(bf16[16,2816]{1,0:T(8,128)(2,1)S(1)} %broadcast_select_fusion.refs_0_), channel_id=1, source_target_pairs={{0,16},{8,24},{16,0},{24,8},{1,17},{9,25},{17,1},{25,9},{2,18},{10... | collective-permute-start | bytes 270344 | tf_op jit(solution)/shard_map/ppermute | solution.py:42
  16.1 0.1 collective-permute-start.26
  16.2 2.1 %state.1 = (f32[1,16,2048]{2,1,0:T(8,128)}, f32[1,16,768]{2,1,0:T(8,128)}, f32[1,16,2048]{2,1,0:T(8,128)}, f32[1,16,768]{2,1,0:T(8,128)}, f32[1,16,2048]{2,1,0:T...) custom-call(bf16[1,768,4096]{2,1,0:T(8,128)(2,1)} %refs_3_.3, f32[16,2816]{1,0:T(8,128)S(1)} %get-tuple-element.78.refs_0_, ...), custom_call_target="tpu_custom_call" | custom-call | bytes 12582912 | tf_op jit(solution)/shard_map/state/pallas_call | solution.py:319
  18.3 0.0 collective-permute-done.28.refs_3_
  18.4 0.4 %collective-permute-done.27.refs_2_ = bf16[16,2816]{1,0:T(8,128)(2,1)S(1)} collective-permute-done((bf16[16,2816]{1,0:T(8,128)(2,1)S(1)}, bf16[16,2816]{1,0:T(8,128)(2,1)S(1)}, u32[]{:S(2)}, u32[]{:S(2)}) %collective-permute-start.27) | collective-permute-done | bytes 90144 | tf_op jit(solution)/shard_map/ppermute | solution.py:42
  18.8 0.7 %collective-permute-done.26.refs_1_ = bf16[16,2816]{1,0:T(8,128)(2,1)S(1)} collective-permute-done((bf16[16,2816]{1,0:T(8,128)(2,1)S(1)}, bf16[16,2816]{1,0:T(8,128)(2,1)S(1)}, u32[]{:S(2)}, u32[]{:S(2)}) %collective-permute-start.26) | collective-permute-done | bytes 90144 | tf_op jit(solution)/shard_map/ppermute | solution.py:42
  19.5 0.1 join.1
  19.6 3.7 %collective-permute-start.29 = (bf16[64,2048]{1,0:T(8,128)(2,1)S(1)}, bf16[64,2048]{1,0:T(8,128)(2,1)S(1)}, u32[]{:S(2)}, u32[]{:S(2)}) collective-permute-start(bf16[64,2048]{1,0:T(8,128)(2,1)S(1)} %get-tuple-element.88.refs_1_), channel_id=1, source_target_pairs={{0,1},{1,0},{2,3},{3,2},{4,5},{5,4},{6,7},{7,6},{8,9},{9,8},{10,11... | collective-permute-start | bytes 786440 | tf_op jit(solution)/shard_map/ppermute | solution.py:42
  23.3 3.3 %merge0.1 = (bf16[1,768,4096]{2,1,0:T(8,128)(2,1)}, bf16[768,2048]{1,0:T(8,128)(2,1)S(1)}) custom-call(bf16[768,2048]{1,0:T(8,128)(2,1)S(1)} %get-tuple-element.87.refs_0_, bf16[64,2048]{1,0:T(8,128)(2,1)S(1)} %get-tuple-element.88.refs_1_, bf16[768,64]{1,0:T(8,128)(2,1)S(1)} %get-tuple-element.89.refs_2_, bf16[1,768,4096]{2,1,0:T(8,128)(2,1)} %refs_3_.3), custom_call_target="tpu_custom_call" | custom-call | flops 201326592 | bytes 3145728 | tf_op jit(solution)/shard_map/merge0/pallas_call | solution.py:354
  26.6 0.0 collective-permute-done.29.refs_1_
  26.7 2.0 %merge1.1 = bf16[1,768,4096]{2,1,0:T(8,128)(2,1)} custom-call(bf16[768,2048]{1,0:T(8,128)(2,1)S(1)} %get-tuple-element.90.refs_0_, bf16[64,2048]{1,0:T(8,128)(2,1)S(1)} %collective-permute-done.29.refs_1_, bf16[768,64]{1,0:T(8,128)(2,1)S(1)} %get-tuple-element.89.refs_2_, bf16[1,768,4096]{2,1,0:T(8,128)(2,1)} %get-tuple-element.91.refs_3_), custom_call_target="tpu_custom_call", output_to_operand_aliasing={{}: (3, {})} | custom-call | flops 201326592 | bytes 3145728 | tf_op jit(solution)/shard_map/merge1/pallas_call | solution.py:354
  (2 shorter events, 0.0 us)
Async XLA Ops:
  1.8 4.3 %collective-permute-start.23 = (bf16[16,2816]{1,0:T(8,128)(2,1)S(1)}, bf16[16,2816]{1,0:T(8,128)(2,1)S(1)}, u32[]{:S(2)}, u32[]{:S(2)}) collective-permute-start(bf16[16,2816]{1,0:T(8,128)(2,1)S(1)} %get-tuple-element.82), channel_id=1, source_target_pairs={{0,24},{8,16},{16,8},{24,0},{1,25},{9,17},{17,9},{25,1},{2,26},{10... | collective-permute-start | bytes 270344 | tf_op jit(solution)/shard_map/ppermute | solution.py:42
  4.0 4.8 %collective-permute-start.24 = (bf16[16,2816]{1,0:T(8,128)(2,1)S(1)}, bf16[16,2816]{1,0:T(8,128)(2,1)S(1)}, u32[]{:S(2)}, u32[]{:S(2)}) collective-permute-start(bf16[16,2816]{1,0:T(8,128)(2,1)S(1)} %get-tuple-element.83), channel_id=1, source_target_pairs={{0,16},{8,24},{16,0},{24,8},{1,17},{9,25},{17,1},{25,9},{2,18},{10... | collective-permute-start | bytes 270344 | tf_op jit(solution)/shard_map/ppermute | solution.py:42
  4.3 4.6 %collective-permute-start.25 = (bf16[16,2816]{1,0:T(8,128)(2,1)S(1)}, bf16[16,2816]{1,0:T(8,128)(2,1)S(1)}, u32[]{:S(2)}, u32[]{:S(2)}) collective-permute-start(bf16[16,2816]{1,0:T(8,128)(2,1)S(1)} %get-tuple-element.84), channel_id=1, source_target_pairs={{0,8},{8,0},{16,24},{24,16},{1,9},{9,1},{17,25},{25,17},{2,10},{10... | collective-permute-start | bytes 270344 | tf_op jit(solution)/shard_map/ppermute | solution.py:42
  9.1 4.3 %collective-permute-start.4 = (bf16[16,2816]{1,0:T(8,128)(2,1)S(1)}, bf16[16,2816]{1,0:T(8,128)(2,1)S(1)}, u32[]{:S(2)}, u32[]{:S(2)}) collective-permute-start(bf16[16,2816]{1,0:T(8,128)(2,1)S(1)} %param.5), channel_id=1, source_target_pairs={{0,1},{1,0},{2,6},{3,7},{4,5},{5,4},{6,2},{7,3},{8,9},{9,8},{10,14... | collective-permute-start | bytes 270344 | tf_op jit(solution)/shard_map/cond/branch_5_fun/ppermute | solution.py:292
  13.5 4.9 %collective-permute-start.28 = (bf16[16,2816]{1,0:T(8,128)(2,1)S(1)}, bf16[16,2816]{1,0:T(8,128)(2,1)S(1)}, u32[]{:S(2)}, u32[]{:S(2)}) collective-permute-start(bf16[16,2816]{1,0:T(8,128)(2,1)S(1)} %broadcast_select_fusion.refs_0_), channel_id=1, source_target_pairs={{0,24},{8,16},{16,8},{24,0},{1,25},{9,17},{17,9},{25,1},{2,26},{10... | collective-permute-start | bytes 270344 | tf_op jit(solution)/shard_map/ppermute | solution.py:42
  14.4 4.4 %collective-permute-start.27 = (bf16[16,2816]{1,0:T(8,128)(2,1)S(1)}, bf16[16,2816]{1,0:T(8,128)(2,1)S(1)}, u32[]{:S(2)}, u32[]{:S(2)}) collective-permute-start(bf16[16,2816]{1,0:T(8,128)(2,1)S(1)} %broadcast_select_fusion.refs_0_), channel_id=1, source_target_pairs={{0,16},{8,24},{16,0},{24,8},{1,17},{9,25},{17,1},{25,9},{2,18},{10... | collective-permute-start | bytes 270344 | tf_op jit(solution)/shard_map/ppermute | solution.py:42
  16.1 3.4 %collective-permute-start.26 = (bf16[16,2816]{1,0:T(8,128)(2,1)S(1)}, bf16[16,2816]{1,0:T(8,128)(2,1)S(1)}, u32[]{:S(2)}, u32[]{:S(2)}) collective-permute-start(bf16[16,2816]{1,0:T(8,128)(2,1)S(1)} %broadcast_select_fusion.refs_0_), channel_id=1, source_target_pairs={{0,8},{8,0},{16,24},{24,16},{1,9},{9,1},{17,25},{25,17},{2,10},{10... | collective-permute-start | bytes 270344 | tf_op jit(solution)/shard_map/ppermute | solution.py:42
  19.6 7.1 %collective-permute-start.29 = (bf16[64,2048]{1,0:T(8,128)(2,1)S(1)}, bf16[64,2048]{1,0:T(8,128)(2,1)S(1)}, u32[]{:S(2)}, u32[]{:S(2)}) collective-permute-start(bf16[64,2048]{1,0:T(8,128)(2,1)S(1)} %get-tuple-element.88.refs_1_), channel_id=1, source_target_pairs={{0,1},{1,0},{2,3},{3,2},{4,5},{5,4},{6,7},{7,6},{8,9},{9,8},{10,11... | collective-permute-start | bytes 786440 | tf_op jit(solution)/shard_map/ppermute | solution.py:42
